TPU v7x, 256 devices: a whole 4x4x8 slice. The times are simulated.
256 devices in a mesh: grp: 16 (over z, core), inner: 16 (over y, x).
Axes of the slice: x: 4, y: 4, z: 8, core: 2. Of those that a mesh axis runs over, the one named last changes fastest.
Arguments:
- snapshots: float32 [64, 2097152], P(None, ('grp', 'inner')), as said below
Outputs:
- basis: float32 [64, 2097152], P(None, ('grp', 'inner'))
- triangle: float32 [64, 64], replicated
Inputs may be any that keep to these rules, and one draw needn't show every extreme that they name: The rows of snapshots are linearly independent.
All inputs are finite; a program needn't handle non-finite values.
Results may differ from a plain program's by a relative error of at most 0.0003.
Values sent between devices are 32-bit elements; how exact they have to be, the bound alone decides.
A program may use at most 64 MiB of HBM per device.

v0:
```python
import math

import jax
import jax.numpy as jnp
from jax import lax
from jax.sharding import PartitionSpec as P

exact_mode = lax.Precision.HIGHEST


def rows_dot(left, right):
    return jnp.einsum("an,bn->ab", left, right, precision=exact_mode)


def householder(panel, offset):
    count, length = panel.shape
    positions = lax.iota(jnp.int32, length)
    slots = lax.iota(jnp.int32, count)

    def one_step(column_at, carry):
        work, vectors, factor = carry
        column = lax.dynamic_index_in_dim(work, column_at, 0, keepdims=False)
        pivot_at = offset + column_at
        masked = jnp.where(positions >= pivot_at, column, 0.0)
        pivot = lax.dynamic_index_in_dim(column, pivot_at, 0, keepdims=False)
        magnitude = jnp.sqrt(jnp.sum(masked * masked))
        alpha = jnp.where(pivot >= 0, -magnitude, magnitude)
        vector = masked - jnp.where(positions == pivot_at, alpha, 0.0)
        tau_value = 2.0 / jnp.sum(vector * vector)
        projected = jnp.dot(work, vector, precision=exact_mode)
        work = work - tau_value * projected[:, None] * vector[None, :]
        correlation = jnp.dot(vectors, vector, precision=exact_mode)
        new_column = -tau_value * jnp.dot(factor, correlation, precision=exact_mode)
        chosen = slots == column_at
        new_column = jnp.where(chosen, tau_value, new_column)
        factor = jnp.where(chosen[None, :], new_column[:, None], factor)
        vectors = lax.dynamic_update_index_in_dim(vectors, vector, column_at, 0)
        return (work, vectors, factor)

    start_state = (
        panel,
        jnp.zeros((count, length), jnp.float32),
        jnp.zeros((count, count), jnp.float32),
    )
    return lax.fori_loop(0, count, one_step, start_state)


def local_factor(snapshots):
    count = snapshots.shape[0]
    width = 16
    rest = snapshots
    tops = []
    reflectors = []
    for start in range(0, count, width):
        panel, vectors, factor = householder(rest[:width], start)
        later = rest[width:]
        if later.shape[0] > 0:
            mixed = jnp.dot(rows_dot(later, vectors), factor, precision=exact_mode)
            later = later - jnp.dot(mixed, vectors, precision=exact_mode)
        tops.append(panel[:, :count])
        reflectors.append((vectors, factor))
        rest = later
    return (jnp.tril(jnp.concatenate(tops, 0)), reflectors)


def form_basis(reflectors, count, length):
    q_rows = jnp.where(
        lax.iota(jnp.int32, length)[None, :] == lax.iota(jnp.int32, count)[:, None], 1.0, 0.0
    ).astype(jnp.float32)
    for vectors, factor in reversed(reflectors):
        mixed = jnp.dot(rows_dot(q_rows, vectors), factor.T, precision=exact_mode)
        q_rows = q_rows - jnp.dot(mixed, vectors, precision=exact_mode)
    return q_rows


def stack_merge(stacked, block_start):
    count = stacked.shape[0]
    work, vectors, factor = householder(stacked, 0)
    r_lower = jnp.tril(work[:, :count])
    coeff = jnp.dot(vectors[:, :count].T, factor.T, precision=exact_mode)
    picked = lax.dynamic_slice_in_dim(vectors, block_start, count, 1)
    identity = jnp.eye(count, dtype=jnp.float32)
    base = jnp.where(block_start == 0, identity, 0.0)
    return (r_lower, base - jnp.dot(coeff, picked, precision=exact_mode))


def tree_passes(snapshots, root):
    count, length = snapshots.shape
    r_lower, reflectors = local_factor(snapshots)
    q_local = form_basis(reflectors, count, length)
    gathered = lax.all_gather(r_lower, "inner", axis=1, tiled=True)
    r_group, b_first = stack_merge(gathered, lax.axis_index("inner") * count)
    gathered_all = lax.all_gather(r_group, "grp", axis=1, tiled=True)
    r_lower, b_second = stack_merge(gathered_all, lax.axis_index("grp") * count)
    b_block = jnp.dot(b_second, b_first, precision=exact_mode)
    signs = jnp.where(jnp.diagonal(r_lower) >= 0, 1.0, -1.0).astype(jnp.float32)
    basis = signs[:, None] * jnp.dot(b_block, q_local, precision=exact_mode) * root
    triangle = signs[:, None] * r_lower.T / root
    return (basis, triangle)


def per_device(snapshots):
    count, length = snapshots.shape
    root = math.sqrt(length * lax.axis_size(("grp", "inner")))
    basis, triangle = tree_passes(snapshots, root)
    return (basis, triangle)


def solution(mesh):
    in_specs = (P(None, ("grp", "inner")),)
    out_specs = (P(None, ("grp", "inner")), P())
    return jax.shard_map(
        per_device, mesh=mesh, in_specs=in_specs, out_specs=out_specs, check_vma=False
    )
```

profile of v0, /device:TPU:1, one launch (start us, length us, event | category | flops | bytes accessed | tf_op | source)
XLA Modules:
  0.0 1206.7 jit_solution(3833780329045786032)
XLA Ops:
  1.8 94.9 %while.132 = (s32[]{:T(128)}, f32[16,8192]{1,0:T(8,128)S(1)}, f32[16,8192]{1,0:T(8,128)S(1)}, f32[16,16]{1,0:T(8,128)S(1)}, s32[]{:T(128)}, /*index=5*/s32[]{:T(...) while((s32[]{:T(128)}, f32[16,8192]{1,0:T(8,128)S(1)}, ...), condition=%wide.region_3.4_spmd.clone.clone, body=%wide.region_0.3_spmd.clone.clone.sunk | while | flops 3526488 | bytes 2576046 | solution.py:45
  96.7 2.9 fusion.87
  102.4 93.9 %while.133 = (s32[]{:T(128)}, f32[16,8192]{1,0:T(8,128)S(1)}, f32[16,8192]{1,0:T(8,128)S(1)}, f32[16,16]{1,0:T(8,128)S(1)}, s32[]{:T(128)}, /*index=5*/s32[]{:T(...) while((s32[]{:T(128)}, f32[16,8192]{1,0:T(8,128)S(1)}, ...), condition=%wide.region_7.8_spmd.clone.clone, body=%wide.region_4.7_spmd.clone.clone.sunk | while | flops 3526492 | bytes 2576108 | solution.py:45
  196.3 2.3 fusion.91
  200.8 93.9 %while.134 = (s32[]{:T(128)}, f32[16,8192]{1,0:T(8,128)S(1)}, f32[16,8192]{1,0:T(8,128)S(1)}, f32[16,16]{1,0:T(8,128)S(1)}, s32[]{:T(128)}, /*index=5*/s32[]{:T(...) while((s32[]{:T(128)}, f32[16,8192]{1,0:T(8,128)S(1)}, ...), condition=%wide.region_11.12_spmd.clone.clone, body=%wide.region_8.11_spmd.clone.clone.sunk | while | flops 3526492 | bytes 2576108 | solution.py:45
  294.7 2.0 fusion.93
  296.8 1.8 convolution_subtract_fusion.6
  299.5 136.2 %while.135 = (s32[]{:T(128)}, f32[16,8192]{1,0:T(8,128)S(1)}, f32[16,8192]{1,0:T(8,128)}, f32[16,16]{1,0:T(8,128)S(1)}, s32[]{:T(128)}, /*index=5*/s32[]{:T(128)...) while((s32[]{:T(128)}, f32[16,8192]{1,0:T(8,128)S(1)}, ...), condition=%wide.region_15.16_spmd.clone.clone, body=%wide.region_12.15_spmd.clone.clone.sunk | while | flops 3526492 | bytes 2576108 | solution.py:45
  304.2 1.7 convolution_bitcast_fusion.27
  306.0 1.8 dynamic_update_slice.89
  312.7 1.7 convolution_bitcast_fusion.27
  314.5 1.8 dynamic_update_slice.89
  321.3 1.7 convolution_bitcast_fusion.27
  323.0 1.8 dynamic_update_slice.89
  329.8 1.7 convolution_bitcast_fusion.27
  331.5 1.8 dynamic_update_slice.89
  338.3 1.7 convolution_bitcast_fusion.27
  340.0 1.8 dynamic_update_slice.89
  346.8 1.7 convolution_bitcast_fusion.27
  348.5 1.8 dynamic_update_slice.89
  355.3 1.7 convolution_bitcast_fusion.27
  357.0 1.8 dynamic_update_slice.89
  365.6 1.8 dynamic_update_slice.89
  374.1 1.8 dynamic_update_slice.89
  382.6 1.8 dynamic_update_slice.89
  391.1 1.8 dynamic_update_slice.89
  399.6 1.8 dynamic_update_slice.89
  408.1 1.8 dynamic_update_slice.89
  416.6 1.8 dynamic_update_slice.89
  425.1 1.8 dynamic_update_slice.89
  433.7 1.8 dynamic_update_slice.89
  435.7 2.6 copy.14
  438.2 2.6 copy.13
  440.9 2.6 copy.12
  443.5 2.6 copy.11
  447.0 19.9 %all_gather.6 = f32[64,1024]{0,1:T(8,128)S(1)} all-gather(f32[64,64]{0,1:T(8,128)S(1)} %maximum_select_fusion), channel_id=1, replica_groups=mesh['grp'=16,'inner'=16] {'inner'}, dimensions={1}, use_global_device_ids=true | all-gather | bytes 278528 | tf_op jit(solution)/shard_map/all_gather | solution.py:91
  467.2 343.9 %while.136 = (s32[]{:T(128)}, f32[64,1024]{1,0:T(8,128)S(1)}, f32[64,1024]{1,0:T(8,128)S(1)}, f32[64,64]{1,0:T(8,128)S(1)}, s32[]{:T(128)}, /*index=5*/s32[]{:T(...) while((s32[]{:T(128)}, f32[64,1024]{1,0:T(8,128)S(1)}, ...), condition=%wide.region_19.20_spmd.clone.clone, body=%wide.region_16.19_spmd.clone.clone.sunk | while | flops 1780040 | bytes 1159054 | solution.py:45
  811.3 27.1 %all_gather.7 = f32[64,1024]{0,1:T(8,128)S(1)} all-gather(f32[64,64]{0,1:T(8,128)S(1)} %slice_select_fusion.1), channel_id=1, replica_groups=mesh['grp'=16,'inner'=16] {'grp'}, dimensions={1}, use_global_device_ids=true | all-gather | bytes 278528 | tf_op jit(solution)/shard_map/all_gather | solution.py:93
  838.6 343.9 %while.137 = (s32[]{:T(128)}, f32[64,1024]{1,0:T(8,128)S(1)}, f32[64,1024]{1,0:T(8,128)S(1)}, f32[64,64]{1,0:T(8,128)S(1)}, s32[]{:T(128)}, /*index=5*/s32[]{:T(...) while((s32[]{:T(128)}, f32[64,1024]{1,0:T(8,128)S(1)}, ...), condition=%wide.region_23.24_spmd.clone.clone, body=%wide.region_20.23_spmd.clone.clone.sunk | while | flops 1780040 | bytes 1159054 | solution.py:45
  1184.2 1.8 fusion.85
  1186.2 1.8 convolution_subtract_fusion.3
  1187.9 1.8 fusion.116
  1189.9 1.8 convolution_subtract_fusion.2
  1191.7 1.8 fusion.118
  1193.6 1.8 convolution_subtract_fusion.1
  1195.4 1.8 fusion.120
  1197.3 3.1 convolution_subtract_fusion
  1201.8 4.9 fusion.84
  (2534 shorter events, 657.9 us)
Async XLA Ops:
  96.7 3.1 copy-start.6
  101.2 1.1 copy-start.3
  196.3 2.4 copy-start.4
  199.8 1.0 copy-start.5
  294.7 2.0 copy-start
  443.5 3.4 slice-start
  443.5 3.4 slice-start.1
  443.5 3.4 slice-start.2
  838.6 345.6 %copy-start.2 = (f32[16,8192]{1,0:T(8,128)S(1)}, f32[16,8192]{1,0:T(8,128)}, u32[]{:S(2)}) copy-start(f32[16,8192]{1,0:T(8,128)} %get-tuple-element.1089) | copy-start | bytes 1572868
  1184.2 3.7 copy-start.1
where the time goes:
time: 1210 us
  loops' own time  420 us (35%)
  other arithmetic  307 us (25%)
  matrix products  235 us (19%)
  local copies, waits for them, and re-layouts  196 us (16%)
  blocking collectives  47 us (4%)
    another operation x6, loops' own time, householder(): return lax.fori_loop(0, count, one_step, start_state)  420 us
    reduce_sum x192, other arithmetic, one_step(): tau_value = 2.0 / jnp.sum(vector * vector)  130 us
    reduce_sum x192, other arithmetic, one_step(): magnitude = jnp.sqrt(jnp.sum(masked * masked))  126 us
    dynamic_slice x192, local copies, waits for them, and re-layouts, one_step(): pivot = lax.dynamic_index_in_dim(column, pivot_at, 0, keepdims=False)  123 us
    dot_general x192, matrix products, one_step(): correlation = jnp.dot(vectors, vector, precision=exact_mode)  95.4 us
    dot_general x192, matrix products, one_step(): projected = jnp.dot(work, vector, precision=exact_mode)  78.9 us
    dynamic_update_slice x192, local copies, waits for them, and re-layouts, one_step(): vectors = lax.dynamic_update_index_in_dim(vectors, vector, column_at, 0)  53.4 us
    all_gather x1, blocking collectives, tree_passes(): gathered_all = lax.all_gather(r_group, 'grp', axis=1, tiled=True)  27.1 us

commit v1 on v0

v1 whole, which is shorter than its diff:
```python
import functools
import math

import jax
import jax.numpy as jnp
from jax import lax
from jax.experimental import pallas as pl
from jax.experimental.pallas import tpu as pltpu
from jax.sharding import PartitionSpec as P

F32 = jnp.float32
BF16 = jnp.bfloat16
EXACT = lax.Precision.HIGHEST
NT = (((1,), (1,)), ((), ()))
NN = (((1,), (0,)), ((), ()))


def two_sum(a, b):
    s = a + b
    t = s - a
    return s, (a - (s - t)) + (b - t)


def quick_two_sum(a, b):
    s = a + b
    return s, b - (s - a)


def power_above(m):
    c = m * 8388609.0
    return 2.0 * (c - (c - m))


def cut(x, scale, exponents):
    pieces = []
    for e in exponents:
        magic = scale * (1.5 * 2.0 ** (23 + e))
        piece = (x + magic) - magic
        x = x - piece
        pieces.append(piece.astype(BF16))
    return pieces, x


def gram_kernel(a_ref, g_ref, h1, e1, h2, e2, x3, y1, y2, y3):
    k = a_ref.shape[0]
    step = pl.program_id(0)

    @pl.when(step == 0)
    def _():
        for ref in (h1, e1, h2, e2, x3, y1, y2, y3):
            ref[...] = jnp.zeros_like(ref)

    x = a_ref[...]
    scale = power_above(jnp.max(jnp.abs(x), axis=1, keepdims=True))
    pieces, _ = cut(x, scale, (-7, -15, -23))
    stack = jnp.concatenate(pieces, axis=0)
    prod = lax.dot_general(stack, stack, NT, preferred_element_type=F32)
    s, e = two_sum(h1[...], prod[:k, : 2 * k])
    h1[...] = s
    e1[...] += e
    s, e = two_sum(h2[...], prod[k : 2 * k, : 2 * k])
    h2[...] = s
    e2[...] += e
    x3[...] += prod[2 * k :, : 2 * k]
    y1[...] += prod[:k, 2 * k :]
    y2[...] += prod[k : 2 * k, 2 * k :]
    y3[...] += prod[2 * k :, 2 * k :]

    @pl.when(step == pl.num_programs(0) - 1)
    def _():
        a1 = h1[...]
        b1 = e1[...]
        a2 = h2[...]
        left = a1[:, :k]
        d2, f2 = two_sum(a1[:, k:], a2[:, :k])
        low = (a2 + x3[...])[:, k:] + x3[:, :k] + y1[...]
        low = low + (b1[:, :k] + b1[:, k:] + e2[:, :k] + y2[...] + y3[...])
        s, f1 = two_sum(left, d2)
        hi, lo = quick_two_sum(s, f1 + f2 + low)
        g_ref[...] = jnp.concatenate([lo, hi], axis=1)


def local_gram(panel):
    k, n = panel.shape
    wide = pltpu.VMEM((k, 2 * k), F32)
    narrow = pltpu.VMEM((k, k), F32)
    block = 1024
    return pl.pallas_call(
        gram_kernel,
        out_shape=jax.ShapeDtypeStruct((k, 2 * k), F32),
        grid=(n // block,),
        in_specs=[pl.BlockSpec((k, block), lambda i: (0, i))],
        out_specs=pl.BlockSpec((k, 2 * k), lambda i: (0, 0)),
        scratch_shapes=[wide, wide, wide, wide, wide, narrow, narrow, narrow],
    )(panel)


def pair_sum(values, k):
    total, err = values[0], None
    for v in values[1:]:
        total, e = two_sum(total, v)
        err = e if err is None else err + e
    lo = total[:, :k] + err[:, k:]
    hi, lo = quick_two_sum(total[:, k:], lo)
    return jnp.concatenate([lo, hi], axis=1)


def sum_kernel(n_inner, n_grp, p_ref, o_ref, part, slot1, mine, slot2, full, send, recv):
    k = p_ref.shape[0]
    rows = k // n_inner
    ii = lax.axis_index("inner")
    gi = lax.axis_index("grp")
    barrier = pltpu.get_barrier_semaphore()
    for d in range(1, n_inner):
        pl.semaphore_signal(
            barrier, inc=1, device_id={"inner": lax.rem(ii + d, n_inner)},
            device_id_type=pl.DeviceIdType.MESH,
        )
    for d in range(1, n_grp):
        pl.semaphore_signal(
            barrier, inc=1, device_id={"grp": lax.rem(gi + d, n_grp)},
            device_id_type=pl.DeviceIdType.MESH,
        )
    for i in range(n_inner):
        part[i] = p_ref[rows * i : rows * (i + 1), :]
    pl.semaphore_wait(barrier, n_inner + n_grp - 2)

    for d in range(1, n_inner):
        to = lax.rem(ii + d, n_inner)
        pltpu.make_async_remote_copy(
            src_ref=part.at[to], dst_ref=slot1.at[d - 1], send_sem=send.at[0],
            recv_sem=recv.at[0], device_id={"inner": to}, device_id_type=pl.DeviceIdType.MESH,
        ).start()
    pltpu.make_async_copy(slot1, slot1, recv.at[0]).wait()
    mine[0] = pair_sum([part[ii]] + [slot1[d] for d in range(n_inner - 1)], k)

    others = slot2.at[pl.ds(0, n_grp - 1)]
    slot2[gi] = mine[0]
    for d in range(1, n_grp):
        to = lax.rem(gi + d, n_grp)
        pltpu.make_async_remote_copy(
            src_ref=mine.at[0], dst_ref=slot2.at[gi], send_sem=send.at[1],
            recv_sem=recv.at[1], device_id={"grp": to}, device_id_type=pl.DeviceIdType.MESH,
        ).start()
    pltpu.make_async_copy(others, others, recv.at[1]).wait()
    final = pair_sum([slot2[g] for g in range(n_grp)], k)
    full[ii] = final
    mine[1] = final

    for d in range(1, n_inner):
        to = lax.rem(ii + d, n_inner)
        pltpu.make_async_remote_copy(
            src_ref=mine.at[1], dst_ref=full.at[ii], send_sem=send.at[2],
            recv_sem=recv.at[2], device_id={"inner": to}, device_id_type=pl.DeviceIdType.MESH,
        ).start()
    pltpu.make_async_copy(slot1, slot1, recv.at[2]).wait()
    for i in range(n_inner):
        o_ref[rows * i : rows * (i + 1), :] = full[i]
    pltpu.make_async_copy(slot1, slot1, send.at[0]).wait()
    pltpu.make_async_copy(others, others, send.at[1]).wait()
    pltpu.make_async_copy(slot1, slot1, send.at[2]).wait()


def device_sum(pairs):
    k, w = pairs.shape
    n_inner, n_grp = lax.axis_size("inner"), lax.axis_size("grp")
    rows = k // n_inner
    vmem = pl.BlockSpec(memory_space=pltpu.VMEM)
    return pl.pallas_call(
        functools.partial(sum_kernel, n_inner, n_grp),
        out_shape=jax.ShapeDtypeStruct((k, w), F32),
        in_specs=[vmem],
        out_specs=vmem,
        scratch_shapes=[
            pltpu.VMEM((n_inner, rows, w), F32),
            pltpu.VMEM((n_inner - 1, rows, w), F32),
            pltpu.VMEM((2, rows, w), F32),
            pltpu.VMEM((n_grp, rows, w), F32),
            pltpu.VMEM((n_inner, rows, w), F32),
            pltpu.SemaphoreType.DMA((3,)),
            pltpu.SemaphoreType.DMA((3,)),
        ],
        compiler_params=pltpu.CompilerParams(collective_id=0, has_side_effects=True),
    )(pairs)


def eliminate(x, k):
    step = 8
    sub = lax.broadcasted_iota(jnp.int32, (step, 2 * k), 0)
    blocks = k // step
    rows = [x[step * i : step * (i + 1), :] for i in range(blocks)]

    def lanes(v, c):
        return jnp.broadcast_to(v[:, c : c + 1], v.shape)

    def row(v, j):
        return jnp.broadcast_to(v[j : j + 1, :], v.shape)

    for b in range(blocks):
        v = rows[b]
        cols = [[lanes(rows[i], k + step * b + j) for j in range(step)] for i in range(b, blocks)]
        scale = None
        for j in range(step):
            pivot = row(cols[0][j], j)
            inv = 1.0 / pivot
            root = lax.rsqrt(pivot)
            scale = root if scale is None else jnp.where(sub == j, root, scale)
            heads = [row(cols[0][m], j) for m in range(j + 1, step)]
            vj = row(v, j)
            for i in range(b, blocks):
                c = cols[i - b]
                mult = c[j] * inv
                if i == b:
                    mult = jnp.where(sub > j, mult, 0.0)
                    v = v - mult * vj
                else:
                    rows[i] = rows[i] - mult * vj
                for m in range(j + 1, step):
                    c[m] = c[m] - mult * heads[m - j - 1]
        rows[b] = v * scale
    return jnp.concatenate(rows, axis=0)


def factor(g, k, norm):
    r_id = lax.broadcasted_iota(jnp.int32, (k, k), 0)
    c_id = lax.broadcasted_iota(jnp.int32, (k, k), 1)
    eye = r_id == c_id
    lo, hi = g[:, :k], g[:, k:]
    diag = jnp.where(eye, hi, 0.0)

    def unit(d):
        c = lax.rsqrt(d)
        c8 = c * 8388609.0
        return c8 - (c8 - c)

    col = unit(jnp.sum(diag, axis=1, keepdims=True))
    row = unit(jnp.sum(diag, axis=0, keepdims=True))
    hi = hi * col * row
    lo = lo * col * row
    ident = jnp.where(eye, 1.0, 0.0).astype(F32)
    w1 = eliminate(jnp.concatenate([ident, hi], axis=1), k)[:, :k]
    w_pieces, _ = cut(w1, power_above(jnp.max(jnp.abs(w1), axis=1, keepdims=True)), (-7, -15))
    w_stack = jnp.concatenate(w_pieces, axis=0)
    w1 = w_pieces[0].astype(F32) + w_pieces[1].astype(F32)
    top, rest = cut(hi, 4.0, (-7, -15, -23))
    tail, _ = cut(rest + lo, 4.0, (-31, -39, -47))
    g_stack = jnp.concatenate(top + tail, axis=0)
    prod = lax.dot_general(g_stack, w_stack, NT, preferred_element_type=F32)
    s, e = prod[:k, :], 0.0
    for i in range(1, 6):
        s, f = two_sum(s, prod[k * i : k * (i + 1), :])
        e = e + f
    u_hi, f = two_sum(s[:, :k], s[:, k:])
    u_hi, u_lo = quick_two_sum(u_hi, f + e[:, :k] + e[:, k:])
    u_scale = power_above(jnp.max(jnp.abs(u_hi), axis=0, keepdims=True))
    top, rest = cut(u_hi, u_scale, (-7, -15, -23))
    tail, _ = cut(rest + u_lo, u_scale, (-31, -39))
    m_hi, m_lo = None, 0.0
    for piece in top + tail:
        prod = lax.dot_general(w_stack, piece, NN, preferred_element_type=F32)
        for part in (prod[:k, :], prod[k:, :]):
            if m_hi is None:
                m_hi = part
            else:
                m_hi, f = two_sum(m_hi, part)
                m_lo = m_lo + f
    m = m_hi + m_lo
    w2 = eliminate(jnp.concatenate([ident, m], axis=1), k)[:, :k]
    w = lax.dot_general(w2, w1, NN, precision=EXACT, preferred_element_type=F32)
    tri = lax.dot_general(w2, u_hi, NT, precision=EXACT, preferred_element_type=F32)
    w = w * (row * norm)
    tri = jnp.where(c_id >= r_id, tri / (row * norm), 0.0)
    return w, tri


def split3(x):
    a = x.astype(BF16)
    x = x - a.astype(F32)
    b = x.astype(BF16)
    return a, b, (x - b.astype(F32)).astype(BF16)


def apply_kernel(norm, g_ref, a_ref, q_ref, t_ref, w_ref):
    k = g_ref.shape[0]

    @pl.when(pl.program_id(0) == 0)
    def _():
        w, tri = factor(g_ref[...], k, norm)
        t_ref[...] = tri
        w0, w1, w2 = split3(w)
        w_ref[...] = jnp.concatenate([w0, w1, w0, w1, w0, w2], axis=1)

    a0, a1, a2 = split3(a_ref[...])
    stack = jnp.concatenate([a0, a0, a1, a1, a2, a0], axis=0)
    q_ref[...] = lax.dot_general(w_ref[...], stack, NN, preferred_element_type=F32)


def factor_and_apply(g, panel, norm):
    k, n = panel.shape
    block = 2048
    return pl.pallas_call(
        functools.partial(apply_kernel, norm),
        out_shape=(jax.ShapeDtypeStruct((k, n), F32), jax.ShapeDtypeStruct((k, k), F32)),
        grid=(n // block,),
        in_specs=[
            pl.BlockSpec((k, 2 * k), lambda i: (0, 0)),
            pl.BlockSpec((k, block), lambda i: (0, i)),
        ],
        out_specs=(
            pl.BlockSpec((k, block), lambda i: (0, i)),
            pl.BlockSpec((k, k), lambda i: (0, 0)),
        ),
        scratch_shapes=[pltpu.VMEM((k, 6 * k), BF16)],
    )(g, panel)


def per_device(panel):
    n_all = panel.shape[1] * lax.axis_size("inner") * lax.axis_size("grp")
    pairs = local_gram(panel)
    total = device_sum(pairs)
    return factor_and_apply(total, panel, math.sqrt(n_all))


def solution(mesh):
    return jax.shard_map(
        per_device,
        mesh=mesh,
        in_specs=(P(None, ("grp", "inner")),),
        out_specs=(P(None, ("grp", "inner")), P()),
        check_vma=False,
    )
```

time: 1210 us -> 43.1 us (0.04)
  loops' own time: 420 us -> 0 us
  other arithmetic: 307 us -> 0 us
  matrix products: 235 us -> 0 us
  local copies, waits for them, and re-layouts: 196 us -> 0 us
  blocking collectives: 47 us -> 0 us
  Pallas kernels: 0 us -> 42.2 us
    another operation x6 -> x0, loops' own time: 420 us -> none  [householder(): return lax.fori_loop(0, count, one_step, start_state)]
    reduce_sum x384 -> x0, other arithmetic: 256 us -> none  [the longest x192 130 us: one_step(): tau_value = 2.0 / jnp.sum(vector * vector)]
    dot_general x603 -> x0, matrix products: 235 us -> none  [the longest x192 95.4 us: one_step(): correlation = jnp.dot(vectors, vector, precision=exact_mode)]
    dynamic_slice x384 -> x0, local copies, waits for them, and re-layouts: 126 us -> none  [the longest x192 123 us: one_step(): pivot = lax.dynamic_index_in_dim(column, pivot_at, 0, keepdims=False)]
    dynamic_update_slice x192 -> x0, local copies, waits for them, and re-layouts: 53.4 us -> none  [one_step(): vectors = lax.dynamic_update_index_in_dim(vectors, vector, column_at, 0)]
    all_gather x2 -> x0, blocking collectives: 47 us -> none  [the longest x1 27.1 us: tree_passes(): gathered_all = lax.all_gather(r_group, 'grp', axis=1, tiled=True)]
    pallas_call x0 -> x3, Pallas kernels: none -> 42.2 us  [the longest x1 25.9 us: device_sum(): pl.pallas_call(functools.partial(sum_kernel, n_inner, n_grp), out_shape=j...]
    sub x384 -> x0, other arithmetic: 28.8 us -> none  [the longest x192 22.1 us: one_step(): work = work - tau_value * projected[:, None] * vector[None, :]]
where the time goes in v1:
time: 43.1 us; the launch traced here: 42.8 us
  Pallas kernels  42.2 us (98%)
  between operations  0.64 us (1%)
    pallas_call x1, Pallas kernels, device_sum(): pl.pallas_call(functools.partial(sum_kernel, n_inner, n_grp), out_shape=j...  25.9 us
    pallas_call x1, Pallas kernels, factor_and_apply(): pl.pallas_call(functools.partial(apply_kernel, norm), out_shape=(jax.Shap...  9.42 us
    pallas_call x1, Pallas kernels, local_gram(): pl.pallas_call(gram_kernel, out_shape=jax.ShapeDtypeStruct((k, 2 * k), F3...  6.84 us

profile of v1, /device:TPU:1, one launch (start us, length us, event | category | flops | bytes accessed | tf_op | source)
XLA Modules:
  0.0 42.8 jit_solution(8184076783976429645)
XLA Ops:
  0.6 6.8 %shard_map.30.p_ref = f32[64,128]{1,0:T(8,128)} custom-call(f32[64,8192]{1,0:T(8,128)} %a_ref.3), custom_call_target="tpu_custom_call" | custom-call | tf_op jit(solution)/shard_map/pallas_call | solution.py:88
  7.5 25.9 %shard_map.31.g_ref = f32[64,128]{1,0:T(8,128)} custom-call(f32[64,128]{1,0:T(8,128)} %shard_map.30.p_ref), custom_call_target="tpu_custom_call" | custom-call | tf_op jit(solution)/shard_map/pallas_call | solution.py:169
  33.4 9.4 %shard_map.32 = (f32[64,8192]{1,0:T(8,128)}, f32[64,64]{1,0:T(8,128)}) custom-call(f32[64,128]{1,0:T(8,128)} %shard_map.31.g_ref, f32[64,8192]{1,0:T(8,128)} %a_ref.3), custom_call_target="tpu_custom_call" | custom-call | tf_op jit(solution)/shard_map/pallas_call | solution.py:301

commit v2 on v1

v2 whole, which is shorter than its diff:
```python
import functools
import math

import jax
import jax.numpy as jnp
from jax import lax
from jax.experimental import pallas as pl
from jax.experimental.pallas import tpu as pltpu
from jax.sharding import PartitionSpec as P

F32 = jnp.float32
BF16 = jnp.bfloat16
EXACT = lax.Precision.HIGHEST
NT = (((1,), (1,)), ((), ()))
NN = (((1,), (0,)), ((), ()))


def two_sum(a, b):
    s = a + b
    t = s - a
    return s, (a - (s - t)) + (b - t)


def quick_two_sum(a, b):
    s = a + b
    return s, b - (s - a)


def power_above(m):
    c = m * 8388609.0
    return 2.0 * (c - (c - m))


def cut(x, scale, exponents):
    pieces = []
    for e in exponents:
        magic = scale * (1.5 * 2.0 ** (23 + e))
        piece = (x + magic) - magic
        x = x - piece
        pieces.append(piece.astype(BF16))
    return pieces, x


QUAD = 4
BLOCK = 1024


def local_gram(blocks, k):
    hi = err = low = None
    for x in blocks:
        scale = power_above(jnp.max(jnp.abs(x), axis=1, keepdims=True))
        pieces, _ = cut(x, scale, (-7, -15, -23))
        stack = jnp.concatenate(pieces, axis=0)
        prod = lax.dot_general(stack, stack, NT, preferred_element_type=F32)
        wide = [prod[k * i : k * (i + 1), : 2 * k] for i in range(3)]
        side = [prod[k * i : k * (i + 1), 2 * k :] for i in range(3)]
        if hi is None:
            hi, low = wide[:2], [wide[2], side[0] + side[1] + side[2]]
            err = [jnp.zeros_like(h) for h in hi]
        else:
            for i in range(2):
                hi[i], e = two_sum(hi[i], wide[i])
                err[i] = err[i] + e
            low = [low[0] + wide[2], low[1] + (side[0] + side[1] + side[2])]
    d, f = two_sum(hi[0][:, k:], hi[1][:, :k])
    rest = (hi[1] + low[0] + err[0])[:, k:] + (low[0] + err[0] + err[1])[:, :k] + low[1]
    s, e = two_sum(hi[0][:, :k], d)
    top, rest = quick_two_sum(s, e + f + rest)
    return jnp.concatenate([rest, top], axis=1)


def fold(x, k):
    h = k // 2
    r_id = lax.broadcasted_iota(jnp.int32, (h, 2 * k), 0)
    c_id = lax.rem(lax.broadcasted_iota(jnp.int32, (h, 2 * k), 1), k)
    low = x[h:, :]
    body = jnp.where(c_id >= r_id, x[:h, :], pltpu.roll(low, 2 * k - h, 1))
    diag = jnp.sum(jnp.where(c_id == r_id + h, low, 0.0), axis=0, keepdims=True)
    return body, diag


def unfold(p, k):
    h = k // 2
    r_id = lax.broadcasted_iota(jnp.int32, (h, 2 * k), 0)
    c_id = lax.rem(lax.broadcasted_iota(jnp.int32, (h, 2 * k), 1), k)
    body = p[:h, :]
    top = jnp.where(c_id >= r_id, body, 0.0)
    low = jnp.where(c_id < r_id + h, jnp.where(c_id >= h, pltpu.roll(body, h, 1), 0.0), 0.0)
    low = jnp.where(c_id == r_id + h, p[h : h + 1, :], low)
    full = jnp.concatenate([top, low], axis=0)
    flip = jnp.concatenate([full, jnp.zeros_like(full)], axis=0).T
    off = lax.broadcasted_iota(jnp.int32, (k, k), 0) != lax.broadcasted_iota(jnp.int32, (k, k), 1)
    lo = full[:, :k] + jnp.where(off, flip[:k, :k], 0.0)
    hi = full[:, k:] + jnp.where(off, flip[k:, :k], 0.0)
    return quick_two_sum(hi, lo)


def pair_sum(ref, count, k):
    total, err = two_sum(ref[0], ref[1])
    for i in range(2, count):
        total, e = two_sum(total, ref[i])
        err = err + e
    err = err[..., k:]
    return total + jnp.concatenate([err, jnp.zeros_like(err)], axis=-1)


def sum_kernel(
    n_inner, n_grp, a_ref, o_ref, panel, in_1, grp_1, grp_2, in_2, load, send, recv
):
    k, n = a_ref.shape
    count = n // BLOCK
    ii = lax.axis_index("inner")
    gi = lax.axis_index("grp")
    loads = []
    for b in range(count):
        at = pl.ds(BLOCK * b, BLOCK)
        loads.append(pltpu.make_async_copy(a_ref.at[:, at], panel.at[:, at], load.at[b]))
        loads[-1].start()

    inner = [{"inner": lax.rem(ii + d, n_inner)} for d in range(1, n_inner)]
    grp = [{"grp": lax.rem(gi + d, n_grp)} for d in range(1, n_grp)]
    mesh_id = pl.DeviceIdType.MESH
    barrier = pltpu.get_barrier_semaphore()
    for to in inner + grp:
        pl.semaphore_signal(barrier, inc=1, device_id=to, device_id_type=mesh_id)

    def blocks():
        for b in range(count):
            loads[b].wait()
            yield panel[:, BLOCK * b : BLOCK * (b + 1)]

    body, diag = fold(local_gram(blocks(), k), k)
    n_a, n_b = in_1.shape[1], grp_1.shape[1]
    for q in range(n_b):
        grp_1[gi, q] = body[QUAD * q : QUAD * (q + 1), :]
    for q in range(n_a - 1):
        in_1[ii, q] = body[QUAD * (n_b + q) : QUAD * (n_b + q + 1), :]
    in_1[ii, n_a - 1] = jnp.broadcast_to(diag, (QUAD, 2 * k))
    pl.semaphore_wait(barrier, n_inner + n_grp - 2)

    def share(slots, me, partners, s):
        for to in partners:
            pltpu.make_async_remote_copy(
                src_ref=slots.at[me], dst_ref=slots.at[me], send_sem=send.at[s],
                recv_sem=recv.at[s], device_id=to, device_id_type=mesh_id,
            ).start()

    def drain(slots, partners, sem):
        others = slots.at[pl.ds(0, len(partners))]
        pltpu.make_async_copy(others, others, sem).wait()

    share(in_1, ii, inner, 0)
    share(grp_1, gi, grp, 1)
    drain(in_1, inner, recv.at[0])
    grp_2[gi] = pair_sum(in_1, n_inner, k)
    share(grp_2, gi, grp, 2)
    drain(grp_1, grp, recv.at[1])
    in_2[ii] = pair_sum(grp_1, n_grp, k)
    share(in_2, ii, inner, 3)
    drain(grp_2, grp, recv.at[2])
    last = pair_sum(grp_2, n_grp, k)
    for q in range(n_a):
        o_ref[QUAD * (n_b + q) : QUAD * (n_b + q + 1), :] = last[q]
    drain(in_2, inner, recv.at[3])
    last = pair_sum(in_2, n_inner, k)
    for q in range(n_b):
        o_ref[QUAD * q : QUAD * (q + 1), :] = last[q]
    drain(in_1, inner, send.at[0])
    drain(grp_1, grp, send.at[1])
    drain(grp_2, grp, send.at[2])
    drain(in_2, inner, send.at[3])


def gram_sum(panel):
    k, n = panel.shape
    n_inner, n_grp = lax.axis_size("inner"), lax.axis_size("grp")
    rows = k // 2 + QUAD
    n_b = rows // QUAD // 2
    n_a = rows // QUAD - n_b
    return pl.pallas_call(
        functools.partial(sum_kernel, n_inner, n_grp),
        out_shape=jax.ShapeDtypeStruct((rows, 2 * k), F32),
        in_specs=[pl.BlockSpec(memory_space=pl.ANY)],
        out_specs=pl.BlockSpec(memory_space=pltpu.VMEM),
        scratch_shapes=[
            pltpu.VMEM((k, n), F32),
            pltpu.VMEM((n_inner, n_a, QUAD, 2 * k), F32),
            pltpu.VMEM((n_grp, n_b, QUAD, 2 * k), F32),
            pltpu.VMEM((n_grp, n_a, QUAD, 2 * k), F32),
            pltpu.VMEM((n_inner, n_b, QUAD, 2 * k), F32),
            pltpu.SemaphoreType.DMA((n // BLOCK,)),
            pltpu.SemaphoreType.DMA((4,)),
            pltpu.SemaphoreType.DMA((4,)),
        ],
        compiler_params=pltpu.CompilerParams(
            collective_id=0, has_side_effects=True, vmem_limit_bytes=32 << 20
        ),
    )(panel)


def eliminate(x, k):
    step = 8
    sub = lax.broadcasted_iota(jnp.int32, (step, 2 * k), 0)
    blocks = k // step
    rows = [x[step * i : step * (i + 1), :] for i in range(blocks)]

    def lanes(v, c):
        return jnp.broadcast_to(v[:, c : c + 1], v.shape)

    def row(v, j):
        return jnp.broadcast_to(v[j : j + 1, :], v.shape)

    for b in range(blocks):
        v = rows[b]
        cols = [[lanes(rows[i], k + step * b + j) for j in range(step)] for i in range(b, blocks)]
        scale = None
        for j in range(step):
            pivot = row(cols[0][j], j)
            inv = 1.0 / pivot
            root = lax.rsqrt(pivot)
            scale = root if scale is None else jnp.where(sub == j, root, scale)
            heads = [row(cols[0][m], j) for m in range(j + 1, step)]
            vj = row(v, j)
            for i in range(b, blocks):
                c = cols[i - b]
                mult = c[j] * inv
                if i == b:
                    mult = jnp.where(sub > j, mult, 0.0)
                    v = v - mult * vj
                else:
                    rows[i] = rows[i] - mult * vj
                for m in range(j + 1, step):
                    c[m] = c[m] - mult * heads[m - j - 1]
        rows[b] = v * scale
    return jnp.concatenate(rows, axis=0)


def factor(packed, k, norm):
    r_id = lax.broadcasted_iota(jnp.int32, (k, k), 0)
    c_id = lax.broadcasted_iota(jnp.int32, (k, k), 1)
    eye = r_id == c_id
    hi, lo = unfold(packed, k)
    diag = jnp.where(eye, hi, 0.0)

    def unit(d):
        c = lax.rsqrt(d)
        c8 = c * 8388609.0
        return c8 - (c8 - c)

    col = unit(jnp.sum(diag, axis=1, keepdims=True))
    row = unit(jnp.sum(diag, axis=0, keepdims=True))
    hi = hi * col * row
    lo = lo * col * row
    ident = jnp.where(eye, 1.0, 0.0).astype(F32)
    w1 = eliminate(jnp.concatenate([ident, hi], axis=1), k)[:, :k]
    w_pieces, _ = cut(w1, power_above(jnp.max(jnp.abs(w1), axis=1, keepdims=True)), (-7, -15))
    w_stack = jnp.concatenate(w_pieces, axis=0)
    w1 = w_pieces[0].astype(F32) + w_pieces[1].astype(F32)
    top, rest = cut(hi, 4.0, (-7, -15, -23))
    tail, _ = cut(rest + lo, 4.0, (-31, -39, -47))
    g_stack = jnp.concatenate(top + tail, axis=0)
    prod = lax.dot_general(g_stack, w_stack, NT, preferred_element_type=F32)
    s, e = prod[:k, :], 0.0
    for i in range(1, 6):
        s, f = two_sum(s, prod[k * i : k * (i + 1), :])
        e = e + f
    u_hi, f = two_sum(s[:, :k], s[:, k:])
    u_hi, u_lo = quick_two_sum(u_hi, f + e[:, :k] + e[:, k:])
    u_scale = power_above(jnp.max(jnp.abs(u_hi), axis=0, keepdims=True))
    top, rest = cut(u_hi, u_scale, (-7, -15, -23))
    tail, _ = cut(rest + u_lo, u_scale, (-31, -39))
    m_hi, m_lo = None, 0.0
    for piece in top + tail:
        prod = lax.dot_general(w_stack, piece, NN, preferred_element_type=F32)
        for part in (prod[:k, :], prod[k:, :]):
            if m_hi is None:
                m_hi = part
            else:
                m_hi, f = two_sum(m_hi, part)
                m_lo = m_lo + f
    m = m_hi + m_lo
    w2 = eliminate(jnp.concatenate([ident, m], axis=1), k)[:, :k]
    w = lax.dot_general(w2, w1, NN, precision=EXACT, preferred_element_type=F32)
    tri = lax.dot_general(w2, u_hi, NT, precision=EXACT, preferred_element_type=F32)
    w = w * (row * norm)
    tri = jnp.where(c_id >= r_id, tri / (row * norm), 0.0)
    return w, tri


def split3(x):
    a = x.astype(BF16)
    x = x - a.astype(F32)
    b = x.astype(BF16)
    return a, b, (x - b.astype(F32)).astype(BF16)


def apply_kernel(norm, g_ref, a_ref, q_ref, t_ref, w_ref):
    k = a_ref.shape[0]

    @pl.when(pl.program_id(0) == 0)
    def _():
        w, tri = factor(g_ref[...], k, norm)
        t_ref[...] = tri
        w0, w1, w2 = split3(w)
        w_ref[...] = jnp.concatenate([w0, w1, w0, w1, w0, w2], axis=1)

    a0, a1, a2 = split3(a_ref[...])
    stack = jnp.concatenate([a0, a0, a1, a1, a2, a0], axis=0)
    q_ref[...] = lax.dot_general(w_ref[...], stack, NN, preferred_element_type=F32)


def factor_and_apply(g, panel, norm):
    k, n = panel.shape
    block = 4096
    return pl.pallas_call(
        functools.partial(apply_kernel, norm),
        out_shape=(jax.ShapeDtypeStruct((k, n), F32), jax.ShapeDtypeStruct((k, k), F32)),
        grid=(n // block,),
        in_specs=[
            pl.BlockSpec(g.shape, lambda i: (0, 0)),
            pl.BlockSpec((k, block), lambda i: (0, i)),
        ],
        out_specs=(
            pl.BlockSpec((k, block), lambda i: (0, i)),
            pl.BlockSpec((k, k), lambda i: (0, 0)),
        ),
        scratch_shapes=[pltpu.VMEM((k, 6 * k), BF16)],
        compiler_params=pltpu.CompilerParams(vmem_limit_bytes=32 << 20),
    )(g, panel)


def per_device(panel):
    n_all = panel.shape[1] * lax.axis_size("inner") * lax.axis_size("grp")
    return factor_and_apply(gram_sum(panel), panel, math.sqrt(n_all))


def solution(mesh):
    return jax.shard_map(
        per_device,
        mesh=mesh,
        in_specs=(P(None, ("grp", "inner")),),
        out_specs=(P(None, ("grp", "inner")), P()),
        check_vma=False,
    )
```

time: 43.1 us -> 34.2 us (0.79)
  Pallas kernels: 42.2 us -> 31.9 us
  local copies, waits for them, and re-layouts: 0 us -> 1.58 us
    pallas_call x2 -> x1, Pallas kernels: 32.7 us -> 24.3 us  [gram_sum(): pl.pallas_call(functools.partial(sum_kernel, n_inner, n_grp), out_shape=j...]
    pallas_call x1, Pallas kernels: 9.42 us -> 7.58 us  [factor_and_apply(): pl.pallas_call(functools.partial(apply_kernel, norm), out_shape=(jax.Shap...]
    unnamed x0 -> x2, local copies, waits for them, and re-layouts: none -> 1.58 us
where the time goes in v2:
time: 34.2 us; the launch traced here: 34.1 us
  Pallas kernels  31.9 us (93%)
  local copies, waits for them, and re-layouts  1.58 us (5%)
  between operations  0.65 us (2%)
    pallas_call x1, Pallas kernels, gram_sum(): pl.pallas_call(functools.partial(sum_kernel, n_inner, n_grp), out_shape=j...  24.3 us
    pallas_call x1, Pallas kernels, factor_and_apply(): pl.pallas_call(functools.partial(apply_kernel, norm), out_shape=(jax.Shap...  7.58 us
    unnamed x2, local copies, waits for them, and re-layouts  1.58 us

profile of v2, /device:TPU:1, one launch (start us, length us, event | category | flops | bytes accessed | tf_op | source)
XLA Modules:
  0.0 34.1 jit_solution(2216630262625452220)
XLA Ops:
  0.6 0.0 copy-start
  0.6 1.6 %copy-done = f32[64,8192]{1,0:T(8,128)S(1)} copy-done((f32[64,8192]{1,0:T(8,128)S(1)}, f32[64,8192]{1,0:T(8,128)}, u32[]{:S(2)}) %copy-start) | copy-done | bytes 2097176
  2.2 24.3 %shard_map.30.g_ref = f32[36,128]{1,0:T(8,128)S(1)} custom-call(f32[64,8192]{1,0:T(8,128)S(1)} %copy-done), custom_call_target="tpu_custom_call" | custom-call | tf_op jit(solution)/shard_map/pallas_call | solution.py:180
  26.5 7.6 %shard_map.31 = (f32[64,8192]{1,0:T(8,128)}, f32[64,64]{1,0:T(8,128)}) custom-call(f32[36,128]{1,0:T(8,128)S(1)} %shard_map.30.g_ref, f32[64,8192]{1,0:T(8,128)S(1)} %copy-done), custom_call_target="tpu_custom_call" | custom-call | tf_op jit(solution)/shard_map/pallas_call | solution.py:315
Async XLA Ops:
  0.6 1.6 %copy-start = (f32[64,8192]{1,0:T(8,128)S(1)}, f32[64,8192]{1,0:T(8,128)}, u32[]{:S(2)}) copy-start(f32[64,8192]{1,0:T(8,128)} %a_ref.3) | copy-start | bytes 6291460

commit v3 on v2

--- a/solution.py
+++ b/solution.py
@@ -43,28 +43,30 @@
 
 QUAD = 4
 BLOCK = 1024
-
-
-def local_gram(blocks, k):
-    hi = err = low = None
-    for x in blocks:
-        scale = power_above(jnp.max(jnp.abs(x), axis=1, keepdims=True))
-        pieces, _ = cut(x, scale, (-7, -15, -23))
-        stack = jnp.concatenate(pieces, axis=0)
-        prod = lax.dot_general(stack, stack, NT, preferred_element_type=F32)
-        wide = [prod[k * i : k * (i + 1), : 2 * k] for i in range(3)]
-        side = [prod[k * i : k * (i + 1), 2 * k :] for i in range(3)]
-        if hi is None:
-            hi, low = wide[:2], [wide[2], side[0] + side[1] + side[2]]
-            err = [jnp.zeros_like(h) for h in hi]
-        else:
-            for i in range(2):
-                hi[i], e = two_sum(hi[i], wide[i])
-                err[i] = err[i] + e
-            low = [low[0] + wide[2], low[1] + (side[0] + side[1] + side[2])]
-    d, f = two_sum(hi[0][:, k:], hi[1][:, :k])
-    rest = (hi[1] + low[0] + err[0])[:, k:] + (low[0] + err[0] + err[1])[:, :k] + low[1]
-    s, e = two_sum(hi[0][:, :k], d)
+LOADS = 2
+STORES = 4
+
+
+def add_products(x, sums, k):
+    hi_0, hi_1, err_0, err_1, low, side = sums
+    scale = power_above(jnp.max(jnp.abs(x), axis=1, keepdims=True))
+    pieces, _ = cut(x, scale, (-7, -15, -23))
+    stack = jnp.concatenate(pieces, axis=0)
+    prod = lax.dot_general(stack, stack, NT, preferred_element_type=F32)
+    hi_0, e = two_sum(hi_0, prod[:k, : 2 * k])
+    err_0 = err_0 + e
+    hi_1, e = two_sum(hi_1, prod[k : 2 * k, : 2 * k])
+    err_1 = err_1 + e
+    low = low + prod[2 * k :, : 2 * k]
+    side = side + (prod[:k, 2 * k :] + prod[k : 2 * k, 2 * k :] + prod[2 * k :, 2 * k :])
+    return hi_0, hi_1, err_0, err_1, low, side
+
+
+def join_products(sums, k):
+    hi_0, hi_1, err_0, err_1, low, side = sums
+    d, f = two_sum(hi_0[:, k:], hi_1[:, :k])
+    rest = (hi_1 + low + err_0)[:, k:] + (low + err_0 + err_1)[:, :k] + side
+    s, e = two_sum(hi_0[:, :k], d)
     top, rest = quick_two_sum(s, e + f + rest)
     return jnp.concatenate([rest, top], axis=1)
 
@@ -108,14 +110,16 @@
     n_inner, n_grp, a_ref, o_ref, panel, in_1, grp_1, grp_2, in_2, load, send, recv
 ):
     k, n = a_ref.shape
-    count = n // BLOCK
+    width = n // LOADS
     ii = lax.axis_index("inner")
     gi = lax.axis_index("grp")
-    loads = []
-    for b in range(count):
-        at = pl.ds(BLOCK * b, BLOCK)
-        loads.append(pltpu.make_async_copy(a_ref.at[:, at], panel.at[:, at], load.at[b]))
-        loads[-1].start()
+
+    def arrival(b):
+        at = pl.ds(width * b, width)
+        return pltpu.make_async_copy(a_ref.at[:, at], panel.at[b], load.at[b])
+
+    for b in range(LOADS):
+        arrival(b).start()
 
     inner = [{"inner": lax.rem(ii + d, n_inner)} for d in range(1, n_inner)]
     grp = [{"grp": lax.rem(gi + d, n_grp)} for d in range(1, n_grp)]
@@ -124,12 +128,15 @@
     for to in inner + grp:
         pl.semaphore_signal(barrier, inc=1, device_id=to, device_id_type=mesh_id)
 
-    def blocks():
-        for b in range(count):
-            loads[b].wait()
-            yield panel[:, BLOCK * b : BLOCK * (b + 1)]
-
-    body, diag = fold(local_gram(blocks(), k), k)
+    def add_copy(b, sums):
+        arrival(b).wait()
+        for c in range(width // BLOCK):
+            sums = add_products(panel[b, :, BLOCK * c : BLOCK * (c + 1)], sums, k)
+        return sums
+
+    zeros = jnp.zeros((k, 2 * k), F32)
+    sums = lax.fori_loop(0, LOADS, add_copy, (zeros,) * 5 + (zeros[:, :k],))
+    body, diag = fold(join_products(sums, k), k)
     n_a, n_b = in_1.shape[1], grp_1.shape[1]
     for q in range(n_b):
         grp_1[gi, q] = body[QUAD * q : QUAD * (q + 1), :]
@@ -180,25 +187,23 @@
     return pl.pallas_call(
         functools.partial(sum_kernel, n_inner, n_grp),
         out_shape=jax.ShapeDtypeStruct((rows, 2 * k), F32),
-        in_specs=[pl.BlockSpec(memory_space=pl.ANY)],
+        in_specs=[pl.BlockSpec(memory_space=pltpu.HBM)],
         out_specs=pl.BlockSpec(memory_space=pltpu.VMEM),
         scratch_shapes=[
-            pltpu.VMEM((k, n), F32),
+            pltpu.VMEM((LOADS, k, n // LOADS), F32),
             pltpu.VMEM((n_inner, n_a, QUAD, 2 * k), F32),
             pltpu.VMEM((n_grp, n_b, QUAD, 2 * k), F32),
             pltpu.VMEM((n_grp, n_a, QUAD, 2 * k), F32),
             pltpu.VMEM((n_inner, n_b, QUAD, 2 * k), F32),
-            pltpu.SemaphoreType.DMA((n // BLOCK,)),
+            pltpu.SemaphoreType.DMA((LOADS,)),
             pltpu.SemaphoreType.DMA((4,)),
             pltpu.SemaphoreType.DMA((4,)),
         ],
-        compiler_params=pltpu.CompilerParams(
-            collective_id=0, has_side_effects=True, vmem_limit_bytes=32 << 20
-        ),
+        compiler_params=pltpu.CompilerParams(collective_id=0, has_side_effects=True),
     )(panel)
 
 
-def eliminate(x, k):
+def eliminate(x, k, beside=None):
     step = 8
     sub = lax.broadcasted_iota(jnp.int32, (step, 2 * k), 0)
     blocks = k // step
@@ -213,29 +218,35 @@
     for b in range(blocks):
         v = rows[b]
         cols = [[lanes(rows[i], k + step * b + j) for j in range(step)] for i in range(b, blocks)]
-        scale = None
-        for j in range(step):
-            pivot = row(cols[0][j], j)
-            inv = 1.0 / pivot
-            root = lax.rsqrt(pivot)
-            scale = root if scale is None else jnp.where(sub == j, root, scale)
-            heads = [row(cols[0][m], j) for m in range(j + 1, step)]
-            vj = row(v, j)
-            for i in range(b, blocks):
-                c = cols[i - b]
-                mult = c[j] * inv
-                if i == b:
-                    mult = jnp.where(sub > j, mult, 0.0)
-                    v = v - mult * vj
-                else:
-                    rows[i] = rows[i] - mult * vj
-                for m in range(j + 1, step):
-                    c[m] = c[m] - mult * heads[m - j - 1]
-        rows[b] = v * scale
+        if beside is not None:
+            beside(b)
+        top = cols[0]
+        diag = None
+        for j in range(0, step, 2):
+            first, cross = row(top[j], j), row(top[j + 1], j)
+            last = row(top[j + 1], j + 1)
+            inv_first = 1.0 / first
+            inv_last = first * (1.0 / (first * last - cross * cross))
+            diag = first if diag is None else jnp.where(sub == j, first, diag)
+            diag = jnp.where(sub == j + 1, last - cross * cross * inv_first, diag)
+            for p, inv in ((j, inv_first), (j + 1, inv_last)):
+                heads = [row(top[m], p) for m in range(p + 1, step)]
+                vp = row(v, p)
+                for i in range(b, blocks):
+                    c = cols[i - b]
+                    mult = c[p] * inv
+                    if i == b:
+                        mult = jnp.where(sub > p, mult, 0.0)
+                        v = v - mult * vp
+                    else:
+                        rows[i] = rows[i] - mult * vp
+                    for m in range(p + 1, step):
+                        c[m] = c[m] - mult * heads[m - p - 1]
+        rows[b] = v * lax.rsqrt(diag)
     return jnp.concatenate(rows, axis=0)
 
 
-def factor(packed, k, norm):
+def first_factor(packed, k, w1_ref, g_ref, unit_ref):
     r_id = lax.broadcasted_iota(jnp.int32, (k, k), 0)
     c_id = lax.broadcasted_iota(jnp.int32, (k, k), 1)
     eye = r_id == c_id
@@ -249,16 +260,24 @@
 
     col = unit(jnp.sum(diag, axis=1, keepdims=True))
     row = unit(jnp.sum(diag, axis=0, keepdims=True))
+    unit_ref[...] = jnp.broadcast_to(row, unit_ref.shape)
     hi = hi * col * row
     lo = lo * col * row
+    top, rest = cut(hi, 4.0, (-7, -15, -23))
+    tail, _ = cut(rest + lo, 4.0, (-31, -39, -47))
+    for i, piece in enumerate(top + tail):
+        g_ref[k * i : k * (i + 1), :] = piece
     ident = jnp.where(eye, 1.0, 0.0).astype(F32)
-    w1 = eliminate(jnp.concatenate([ident, hi], axis=1), k)[:, :k]
+    w1_ref[...] = eliminate(jnp.concatenate([ident, hi], axis=1), k)[:, :k]
+
+
+def factor(w1, g_stack, row, k, norm, beside):
+    r_id = lax.broadcasted_iota(jnp.int32, (k, k), 0)
+    c_id = lax.broadcasted_iota(jnp.int32, (k, k), 1)
+    ident = jnp.where(r_id == c_id, 1.0, 0.0).astype(F32)
     w_pieces, _ = cut(w1, power_above(jnp.max(jnp.abs(w1), axis=1, keepdims=True)), (-7, -15))
     w_stack = jnp.concatenate(w_pieces, axis=0)
     w1 = w_pieces[0].astype(F32) + w_pieces[1].astype(F32)
-    top, rest = cut(hi, 4.0, (-7, -15, -23))
-    tail, _ = cut(rest + lo, 4.0, (-31, -39, -47))
-    g_stack = jnp.concatenate(top + tail, axis=0)
     prod = lax.dot_general(g_stack, w_stack, NT, preferred_element_type=F32)
     s, e = prod[:k, :], 0.0
     for i in range(1, 6):
@@ -279,7 +298,7 @@
                 m_hi, f = two_sum(m_hi, part)
                 m_lo = m_lo + f
     m = m_hi + m_lo
-    w2 = eliminate(jnp.concatenate([ident, m], axis=1), k)[:, :k]
+    w2 = eliminate(jnp.concatenate([ident, m], axis=1), k, beside)[:, :k]
     w = lax.dot_general(w2, w1, NN, precision=EXACT, preferred_element_type=F32)
     tri = lax.dot_general(w2, u_hi, NT, precision=EXACT, preferred_element_type=F32)
     w = w * (row * norm)
@@ -294,38 +313,67 @@
     return a, b, (x - b.astype(F32)).astype(BF16)
 
 
-def apply_kernel(norm, g_ref, a_ref, q_ref, t_ref, w_ref):
-    k = a_ref.shape[0]
-
-    @pl.when(pl.program_id(0) == 0)
-    def _():
-        w, tri = factor(g_ref[...], k, norm)
-        t_ref[...] = tri
-        w0, w1, w2 = split3(w)
-        w_ref[...] = jnp.concatenate([w0, w1, w0, w1, w0, w2], axis=1)
-
-    a0, a1, a2 = split3(a_ref[...])
-    stack = jnp.concatenate([a0, a0, a1, a1, a2, a0], axis=0)
-    q_ref[...] = lax.dot_general(w_ref[...], stack, NN, preferred_element_type=F32)
+def apply_kernel(
+    norm, p_ref, a_ref, q_ref, t_ref, panel, pieces, out, tri, w1, g_stack, unit, load, store
+):
+    k, n = a_ref.shape
+    width = n // LOADS
+    loads = []
+    for b in range(LOADS):
+        at = pl.ds(width * b, width)
+        loads.append(pltpu.make_async_copy(a_ref.at[:, at], panel.at[:, at], load.at[b]))
+        loads[-1].start()
+
+    def one_pass(_, carry):
+        first_factor(p_ref[...], k, w1, g_stack, unit)
+        return carry
+
+    lax.fori_loop(0, jnp.minimum(lax.axis_index("inner") + 1, 1), one_pass, 0)
+    for copy in loads:
+        copy.wait()
+
+    def split_block(b):
+        at = slice(n // 8 * b, n // 8 * (b + 1))
+        for i, piece in enumerate(split3(panel[:, at])):
+            pieces[k * i : k * (i + 1), at] = piece
+
+    w, tri[...] = factor(w1[...], g_stack[...], unit[:1, :], k, norm, split_block)
+    stores = [pltpu.make_async_copy(tri, t_ref, store.at[STORES])]
+    stores[0].start()
+    w0, w1, w2 = split3(w)
+    w = jnp.concatenate([w0, w1, w0, w1, w0, w2], axis=1)
+    width = n // STORES
+    for b in range(STORES):
+        at = pl.ds(width * b, width)
+        a0, a1, a2 = (pieces[k * i : k * (i + 1), at] for i in range(3))
+        stack = jnp.concatenate([a0, a0, a1, a1, a2, a0], axis=0)
+        out[:, at] = lax.dot_general(w, stack, NN, preferred_element_type=F32)
+        stores.append(pltpu.make_async_copy(out.at[:, at], q_ref.at[:, at], store.at[b]))
+        stores[-1].start()
+    for copy in stores:
+        copy.wait()
 
 
 def factor_and_apply(g, panel, norm):
     k, n = panel.shape
-    block = 4096
+    whole = pl.BlockSpec(memory_space=pltpu.VMEM)
+    stay = pl.BlockSpec(memory_space=pltpu.HBM)
     return pl.pallas_call(
         functools.partial(apply_kernel, norm),
         out_shape=(jax.ShapeDtypeStruct((k, n), F32), jax.ShapeDtypeStruct((k, k), F32)),
-        grid=(n // block,),
-        in_specs=[
-            pl.BlockSpec(g.shape, lambda i: (0, 0)),
-            pl.BlockSpec((k, block), lambda i: (0, i)),
+        in_specs=[whole, stay],
+        out_specs=(stay, stay),
+        scratch_shapes=[
+            pltpu.VMEM((k, n), F32),
+            pltpu.VMEM((3 * k, n), BF16),
+            pltpu.VMEM((k, n), F32),
+            pltpu.VMEM((k, k), F32),
+            pltpu.VMEM((k, k), F32),
+            pltpu.VMEM((6 * k, k), BF16),
+            pltpu.VMEM((8, k), F32),
+            pltpu.SemaphoreType.DMA((LOADS,)),
+            pltpu.SemaphoreType.DMA((STORES + 1,)),
         ],
-        out_specs=(
-            pl.BlockSpec((k, block), lambda i: (0, i)),
-            pl.BlockSpec((k, k), lambda i: (0, 0)),
-        ),
-        scratch_shapes=[pltpu.VMEM((k, 6 * k), BF16)],
-        compiler_params=pltpu.CompilerParams(vmem_limit_bytes=32 << 20),
     )(g, panel)
 
 

time: 34.2 us -> 32 us (0.936)
  local copies, waits for them, and re-layouts: 1.58 us -> 0 us
  Pallas kernels: 31.9 us -> 31.2 us
    unnamed x2 -> x0, local copies, waits for them, and re-layouts: 1.58 us -> none
    pallas_call x1, Pallas kernels: 24.3 us -> 23.5 us  [gram_sum(): pl.pallas_call(functools.partial(sum_kernel, n_inner, n_grp), out_shape=j...]
where the time goes in v3:
time: 32 us; the launch traced here: 31.8 us
  Pallas kernels  31.2 us (98%)
  between operations  0.64 us (2%)
    pallas_call x1, Pallas kernels, gram_sum(): pl.pallas_call(functools.partial(sum_kernel, n_inner, n_grp), out_shape=j...  23.5 us
    pallas_call x1, Pallas kernels, factor_and_apply(): pl.pallas_call(functools.partial(apply_kernel, norm), out_shape=(jax.Shap...  7.73 us

profile of v3, /device:TPU:1, one launch (start us, length us, event | category | flops | bytes accessed | tf_op | source)
XLA Modules:
  0.0 31.8 jit_solution(8788599540004780391)
XLA Ops:
  0.6 23.5 %shard_map.30.p_ref = f32[36,128]{1,0:T(8,128)} custom-call(f32[64,8192]{1,0:T(8,128)} %a_ref.3), custom_call_target="tpu_custom_call" | custom-call | tf_op jit(solution)/shard_map/pallas_call | solution.py:187
  24.1 7.7 %shard_map.31 = (f32[64,8192]{1,0:T(8,128)}, f32[64,64]{1,0:T(8,128)}) custom-call(f32[36,128]{1,0:T(8,128)} %shard_map.30.p_ref, f32[64,8192]{1,0:T(8,128)} %a_ref.3), custom_call_target="tpu_custom_call" | custom-call | tf_op jit(solution)/shard_map/pallas_call | solution.py:361

commit v4 on v3

--- a/solution.py
+++ b/solution.py
@@ -97,17 +97,21 @@
     return quick_two_sum(hi, lo)
 
 
-def pair_sum(ref, count, k):
-    total, err = two_sum(ref[0], ref[1])
-    for i in range(2, count):
-        total, e = two_sum(total, ref[i])
+def pair_sum(values, k):
+    total, err = two_sum(values[0], values[1])
+    for v in values[2:]:
+        total, e = two_sum(total, v)
         err = err + e
     err = err[..., k:]
     return total + jnp.concatenate([err, jnp.zeros_like(err)], axis=-1)
 
 
+def far_first(n):
+    return sorted(((min(d, n - d), d) for d in range(n)), reverse=True)
+
+
 def sum_kernel(
-    n_inner, n_grp, a_ref, o_ref, panel, in_1, grp_1, grp_2, in_2, load, send, recv
+    n_inner, n_grp, a_ref, o_ref, panel, halves, half, in_1, col_1, col_2, in_2, load, send, recv
 ):
     k, n = a_ref.shape
     width = n // LOADS
@@ -121,11 +125,27 @@
     for b in range(LOADS):
         arrival(b).start()
 
-    inner = [{"inner": lax.rem(ii + d, n_inner)} for d in range(1, n_inner)]
-    grp = [{"grp": lax.rem(gi + d, n_grp)} for d in range(1, n_grp)]
+    side, depth = math.isqrt(n_inner), n_grp // 2
+    y, x = lax.div(ii, side), lax.rem(ii, side)
+    level, core = lax.div(gi, 2), lax.rem(gi, 2)
+    mate = gi + 1 - 2 * core
+    sibling = [(0, {"grp": mate})]
+    plane, plane_mates, column, column_mates = [], [], [], []
+    for far_y, dy in far_first(side):
+        for far_x, dx in far_first(side):
+            if dy or dx:
+                to = lax.rem(y + dy, side) * side + lax.rem(x + dx, side)
+                plane.append((far_y + far_x, {"inner": to}))
+                plane_mates.append((far_y + far_x, {"inner": to, "grp": mate}))
+    for far, d in far_first(depth):
+        if d:
+            to = 2 * lax.rem(level + d, depth)
+            column.append((far, {"grp": to + core}))
+            column_mates.append((far, {"grp": to + 1 - core}))
     mesh_id = pl.DeviceIdType.MESH
     barrier = pltpu.get_barrier_semaphore()
-    for to in inner + grp:
+    everyone = plane_mates + column_mates + plane + column + sibling
+    for _, to in sorted(everyone, key=lambda p: -p[0]):
         pl.semaphore_signal(barrier, inc=1, device_id=to, device_id_type=mesh_id)
 
     def add_copy(b, sums):
@@ -137,53 +157,72 @@
     zeros = jnp.zeros((k, 2 * k), F32)
     sums = lax.fori_loop(0, LOADS, add_copy, (zeros,) * 5 + (zeros[:, :k],))
     body, diag = fold(join_products(sums, k), k)
-    n_a, n_b = in_1.shape[1], grp_1.shape[1]
-    for q in range(n_b):
-        grp_1[gi, q] = body[QUAD * q : QUAD * (q + 1), :]
-    for q in range(n_a - 1):
-        in_1[ii, q] = body[QUAD * (n_b + q) : QUAD * (n_b + q + 1), :]
-    in_1[ii, n_a - 1] = jnp.broadcast_to(diag, (QUAD, 2 * k))
-    pl.semaphore_wait(barrier, n_inner + n_grp - 2)
-
-    def share(slots, me, partners, s):
-        for to in partners:
+    quads = halves.shape[1]
+    n_a, n_b = in_1.shape[1], col_1.shape[1]
+    per_body = k // 2 // QUAD
+    for q in range(2 * quads):
+        if q < per_body:
+            piece = body[QUAD * q : QUAD * (q + 1), :]
+        else:
+            piece = jnp.broadcast_to(diag, (QUAD, 2 * k))
+        halves[q // quads, q % quads] = piece
+    pl.semaphore_wait(barrier, len(everyone))
+
+    def share(*sets):
+        todo = [(far, to, st) for st in sets for far, to in st[2]]
+        for _, to, (source, target, _, s) in sorted(todo, key=lambda p: -p[0]):
             pltpu.make_async_remote_copy(
-                src_ref=slots.at[me], dst_ref=slots.at[me], send_sem=send.at[s],
+                src_ref=source, dst_ref=target, send_sem=send.at[s],
                 recv_sem=recv.at[s], device_id=to, device_id_type=mesh_id,
             ).start()
 
-    def drain(slots, partners, sem):
-        others = slots.at[pl.ds(0, len(partners))]
-        pltpu.make_async_copy(others, others, sem).wait()
-
-    share(in_1, ii, inner, 0)
-    share(grp_1, gi, grp, 1)
-    drain(in_1, inner, recv.at[0])
-    grp_2[gi] = pair_sum(in_1, n_inner, k)
-    share(grp_2, gi, grp, 2)
-    drain(grp_1, grp, recv.at[1])
-    in_2[ii] = pair_sum(grp_1, n_grp, k)
-    share(in_2, ii, inner, 3)
-    drain(grp_2, grp, recv.at[2])
-    last = pair_sum(grp_2, n_grp, k)
-    for q in range(n_a):
-        o_ref[QUAD * (n_b + q) : QUAD * (n_b + q + 1), :] = last[q]
-    drain(in_2, inner, recv.at[3])
-    last = pair_sum(in_2, n_inner, k)
-    for q in range(n_b):
-        o_ref[QUAD * q : QUAD * (q + 1), :] = last[q]
-    drain(in_1, inner, send.at[0])
-    drain(grp_1, grp, send.at[1])
-    drain(grp_2, grp, send.at[2])
-    drain(in_2, inner, send.at[3])
+    def drain(slots, count, sem):
+        some = slots.at[pl.ds(0, count)]
+        pltpu.make_async_copy(some, some, sem).wait()
+
+    share((halves.at[1 - core], half.at[0], sibling, 0))
+    drain(half, 1, recv.at[0])
+    mine = pair_sum([halves[core], half[0]], k)
+    in_1[ii] = mine[:n_a]
+    col_1[level] = mine[n_a:]
+    share((in_1.at[ii], in_1.at[ii], plane, 1), (col_1.at[level], col_1.at[level], column, 2))
+    drain(in_1, n_inner - 1, recv.at[1])
+    col_2[gi] = pair_sum([in_1[i] for i in range(n_inner)], k)
+    share((col_2.at[gi], col_2.at[gi], column + column_mates + sibling, 3))
+    drain(col_1, depth - 1, recv.at[2])
+    place = core * n_inner + ii
+    in_2[place] = pair_sum([col_1[i] for i in range(depth)], k)
+    share((in_2.at[place], in_2.at[place], plane + plane_mates + sibling, 4))
+
+    def put(value, start):
+        for q in range(value.shape[0]):
+            if QUAD * (start + q) < o_ref.shape[0]:
+                o_ref[QUAD * (start + q) : QUAD * (start + q + 1), :] = value[q]
+
+    drain(col_2, n_grp - 1, recv.at[3])
+    for c in range(2):
+        put(pair_sum([col_2[2 * i + c] for i in range(depth)], k), quads * c)
+    drain(in_2, 2 * n_inner - 1, recv.at[4])
+    for c in range(2):
+        put(pair_sum([in_2[n_inner * c + i] for i in range(n_inner)], k), quads * c + n_a)
+    drain(half, 1, send.at[0])
+    drain(in_1, n_inner - 1, send.at[1])
+    drain(col_1, depth - 1, send.at[2])
+    drain(col_2, n_grp - 1, send.at[3])
+    drain(in_2, 2 * n_inner - 1, send.at[4])
 
 
 def gram_sum(panel):
     k, n = panel.shape
     n_inner, n_grp = lax.axis_size("inner"), lax.axis_size("grp")
     rows = k // 2 + QUAD
-    n_b = rows // QUAD // 2
-    n_a = rows // QUAD - n_b
+    quads = -(-rows // (2 * QUAD))
+    n_b = quads // 2
+    n_a = quads - n_b
+
+    def slots(count, size):
+        return pltpu.VMEM((count, size, QUAD, 2 * k), F32)
+
     return pl.pallas_call(
         functools.partial(sum_kernel, n_inner, n_grp),
         out_shape=jax.ShapeDtypeStruct((rows, 2 * k), F32),
@@ -191,13 +230,15 @@
         out_specs=pl.BlockSpec(memory_space=pltpu.VMEM),
         scratch_shapes=[
             pltpu.VMEM((LOADS, k, n // LOADS), F32),
-            pltpu.VMEM((n_inner, n_a, QUAD, 2 * k), F32),
-            pltpu.VMEM((n_grp, n_b, QUAD, 2 * k), F32),
-            pltpu.VMEM((n_grp, n_a, QUAD, 2 * k), F32),
-            pltpu.VMEM((n_inner, n_b, QUAD, 2 * k), F32),
+            slots(2, quads),
+            slots(1, quads),
+            slots(n_inner, n_a),
+            slots(n_grp // 2, n_b),
+            slots(n_grp, n_a),
+            slots(2 * n_inner, n_b),
             pltpu.SemaphoreType.DMA((LOADS,)),
-            pltpu.SemaphoreType.DMA((4,)),
-            pltpu.SemaphoreType.DMA((4,)),
+            pltpu.SemaphoreType.DMA((5,)),
+            pltpu.SemaphoreType.DMA((5,)),
         ],
         compiler_params=pltpu.CompilerParams(collective_id=0, has_side_effects=True),
     )(panel)

time: 32 us -> 31.2 us (0.975)
  Pallas kernels: 31.2 us -> 30.4 us
    pallas_call x1, Pallas kernels: 23.5 us -> 22.6 us  [gram_sum(): pl.pallas_call(functools.partial(sum_kernel, n_inner, n_grp), out_shape=j...]
where the time goes in v4:
time: 31.2 us; the launch traced here: 31 us
  Pallas kernels  30.4 us (97%)
  between operations  0.64 us (2%)
    pallas_call x1, Pallas kernels, gram_sum(): pl.pallas_call(functools.partial(sum_kernel, n_inner, n_grp), out_shape=j...  22.6 us
    pallas_call x1, Pallas kernels, factor_and_apply(): pl.pallas_call(functools.partial(apply_kernel, norm), out_shape=(jax.Shap...  7.72 us

profile of v4, /device:TPU:1, one launch (start us, length us, event | category | flops | bytes accessed | tf_op | source)
XLA Modules:
  0.0 31.0 jit_solution(7592009650517477562)
XLA Ops:
  0.6 22.6 %shard_map.30.p_ref = f32[36,128]{1,0:T(8,128)} custom-call(f32[64,8192]{1,0:T(8,128)} %a_ref.3), custom_call_target="tpu_custom_call" | custom-call | tf_op jit(solution)/shard_map/pallas_call | solution.py:226
  23.3 7.7 %shard_map.31 = (f32[64,8192]{1,0:T(8,128)}, f32[64,64]{1,0:T(8,128)}) custom-call(f32[36,128]{1,0:T(8,128)} %shard_map.30.p_ref, f32[64,8192]{1,0:T(8,128)} %a_ref.3), custom_call_target="tpu_custom_call" | custom-call | tf_op jit(solution)/shard_map/pallas_call | solution.py:402

commit v5 on v4

--- a/solution.py
+++ b/solution.py
@@ -244,7 +244,7 @@
     )(panel)
 
 
-def eliminate(x, k, beside=None):
+def eliminate(x, k):
     step = 8
     sub = lax.broadcasted_iota(jnp.int32, (step, 2 * k), 0)
     blocks = k // step
@@ -259,8 +259,6 @@
     for b in range(blocks):
         v = rows[b]
         cols = [[lanes(rows[i], k + step * b + j) for j in range(step)] for i in range(b, blocks)]
-        if beside is not None:
-            beside(b)
         top = cols[0]
         diag = None
         for j in range(0, step, 2):
@@ -312,34 +310,49 @@
     w1_ref[...] = eliminate(jnp.concatenate([ident, hi], axis=1), k)[:, :k]
 
 
-def factor(w1, g_stack, row, k, norm, beside):
+def half_lower(x, r_id, c_id):
+    return jnp.where(r_id > c_id, x, jnp.where(r_id == c_id, 0.5 * x, 0.0))
+
+
+def factor(w1, g_stack, row, k, norm, w2_ref, beside):
     r_id = lax.broadcasted_iota(jnp.int32, (k, k), 0)
     c_id = lax.broadcasted_iota(jnp.int32, (k, k), 1)
     ident = jnp.where(r_id == c_id, 1.0, 0.0).astype(F32)
-    w_pieces, _ = cut(w1, power_above(jnp.max(jnp.abs(w1), axis=1, keepdims=True)), (-7, -15))
+    w_pieces, _ = cut(w1, power_above(jnp.max(jnp.abs(w1), axis=1, keepdims=True)), (-8, -17))
     w_stack = jnp.concatenate(w_pieces, axis=0)
     w1 = w_pieces[0].astype(F32) + w_pieces[1].astype(F32)
     prod = lax.dot_general(g_stack, w_stack, NT, preferred_element_type=F32)
-    s, e = prod[:k, :], 0.0
-    for i in range(1, 6):
-        s, f = two_sum(s, prod[k * i : k * (i + 1), :])
-        e = e + f
+    beside(0, 3)
+    part = [prod[k * i : k * (i + 1), :] for i in range(6)]
+    s, e = two_sum(part[0], part[1])
+    s, f = two_sum(s, part[2])
+    e = e + f + (part[3] + (part[4] + part[5]))
     u_hi, f = two_sum(s[:, :k], s[:, k:])
     u_hi, u_lo = quick_two_sum(u_hi, f + e[:, :k] + e[:, k:])
     u_scale = power_above(jnp.max(jnp.abs(u_hi), axis=0, keepdims=True))
     top, rest = cut(u_hi, u_scale, (-7, -15, -23))
     tail, _ = cut(rest + u_lo, u_scale, (-31, -39))
-    m_hi, m_lo = None, 0.0
-    for piece in top + tail:
-        prod = lax.dot_general(w_stack, piece, NN, preferred_element_type=F32)
-        for part in (prod[:k, :], prod[k:, :]):
-            if m_hi is None:
-                m_hi = part
-            else:
-                m_hi, f = two_sum(m_hi, part)
-                m_lo = m_lo + f
-    m = m_hi + m_lo
-    w2 = eliminate(jnp.concatenate([ident, m], axis=1), k, beside)[:, :k]
+    part = [lax.dot_general(w_stack, p, NN, preferred_element_type=F32) for p in top + tail]
+    beside(3, 8)
+    large = [part[0][:k], part[0][k:], part[1][:k], part[1][k:], part[2][:k]]
+    m_lo = part[2][k:] + part[3][:k] + (part[3][k:] + part[4][:k] + part[4][k:])
+    m_hi = large[0]
+    for v in large[1:]:
+        m_hi, f = two_sum(m_hi, v)
+        m_lo = m_lo + f
+    rest = (m_hi - ident) + m_lo
+    p = half_lower(rest, r_id, c_id)
+    p_16 = p.astype(BF16)
+    square = lax.dot_general(p_16, p_16, NN, preferred_element_type=F32)
+    gram = lax.dot_general(p_16, p_16, NT, preferred_element_type=F32)
+    w2_ref[...] = ident - p + (square + half_lower(gram, r_id, c_id))
+    small = jnp.sum(p * p) < 2.0**-11
+
+    @pl.when(jnp.logical_not(small))
+    def _():
+        w2_ref[...] = eliminate(jnp.concatenate([ident, ident + rest], axis=1), k)[:, :k]
+
+    w2 = w2_ref[...]
     w = lax.dot_general(w2, w1, NN, precision=EXACT, preferred_element_type=F32)
     tri = lax.dot_general(w2, u_hi, NT, precision=EXACT, preferred_element_type=F32)
     w = w * (row * norm)
@@ -355,7 +368,7 @@
 
 
 def apply_kernel(
-    norm, p_ref, a_ref, q_ref, t_ref, panel, pieces, out, tri, w1, g_stack, unit, load, store
+    norm, p_ref, a_ref, q_ref, t_ref, panel, pieces, out, tri, w1, w2, g_stack, unit, load, store
 ):
     k, n = a_ref.shape
     width = n // LOADS
@@ -373,12 +386,13 @@
     for copy in loads:
         copy.wait()
 
-    def split_block(b):
-        at = slice(n // 8 * b, n // 8 * (b + 1))
-        for i, piece in enumerate(split3(panel[:, at])):
-            pieces[k * i : k * (i + 1), at] = piece
-
-    w, tri[...] = factor(w1[...], g_stack[...], unit[:1, :], k, norm, split_block)
+    def split_blocks(first, last):
+        for b in range(first, last):
+            at = slice(n // 8 * b, n // 8 * (b + 1))
+            for i, piece in enumerate(split3(panel[:, at])):
+                pieces[k * i : k * (i + 1), at] = piece
+
+    w, tri[...] = factor(w1[...], g_stack[...], unit[:1, :], k, norm, w2, split_blocks)
     stores = [pltpu.make_async_copy(tri, t_ref, store.at[STORES])]
     stores[0].start()
     w0, w1, w2 = split3(w)
@@ -410,6 +424,7 @@
             pltpu.VMEM((k, n), F32),
             pltpu.VMEM((k, k), F32),
             pltpu.VMEM((k, k), F32),
+            pltpu.VMEM((k, k), F32),
             pltpu.VMEM((6 * k, k), BF16),
             pltpu.VMEM((8, k), F32),
             pltpu.SemaphoreType.DMA((LOADS,)),

time: 31.2 us -> 32 us (1.026)
  Pallas kernels: 30.4 us -> 31.2 us
    pallas_call x1, Pallas kernels: 7.72 us -> 8.6 us  [factor_and_apply(): pl.pallas_call(functools.partial(apply_kernel, norm), out_shape=(jax.Shap...]
where the time goes in v5:
time: 32 us; the launch traced here: 31.9 us
  Pallas kernels  31.2 us (98%)
  between operations  0.64 us (2%)
    pallas_call x1, Pallas kernels, gram_sum(): pl.pallas_call(functools.partial(sum_kernel, n_inner, n_grp), out_shape=j...  22.6 us
    pallas_call x1, Pallas kernels, factor_and_apply(): pl.pallas_call(functools.partial(apply_kernel, norm), out_shape=(jax.Shap...  8.6 us

profile of v5, /device:TPU:1, one launch (start us, length us, event | category | flops | bytes accessed | tf_op | source)
XLA Modules:
  0.0 31.9 jit_solution(3943818777820093020)
XLA Ops:
  0.6 22.6 %shard_map.30.p_ref = f32[36,128]{1,0:T(8,128)} custom-call(f32[64,8192]{1,0:T(8,128)} %a_ref.3), custom_call_target="tpu_custom_call" | custom-call | tf_op jit(solution)/shard_map/pallas_call | solution.py:226
  23.3 8.6 %shard_map.31 = (f32[64,8192]{1,0:T(8,128)}, f32[64,64]{1,0:T(8,128)}) custom-call(f32[36,128]{1,0:T(8,128)} %shard_map.30.p_ref, f32[64,8192]{1,0:T(8,128)} %a_ref.3), custom_call_target="tpu_custom_call" | custom-call | tf_op jit(solution)/shard_map/pallas_call | solution.py:416

commit v6 on v5

--- a/solution.py
+++ b/solution.py
@@ -44,7 +44,7 @@
 QUAD = 4
 BLOCK = 1024
 LOADS = 2
-STORES = 4
+STORES = 8
 
 
 def add_products(x, sums, k):
@@ -111,7 +111,8 @@
 
 
 def sum_kernel(
-    n_inner, n_grp, a_ref, o_ref, panel, halves, half, in_1, col_1, col_2, in_2, load, send, recv
+    n_inner, n_grp, a_ref, o_ref, s_ref, panel, pieces, halves, half, in_1, col_1, col_2, in_2,
+    load, send, recv, done
 ):
     k, n = a_ref.shape
     width = n // LOADS
@@ -186,6 +187,17 @@
     in_1[ii] = mine[:n_a]
     col_1[level] = mine[n_a:]
     share((in_1.at[ii], in_1.at[ii], plane, 1), (col_1.at[level], col_1.at[level], column, 2))
+
+    def split_panel(_, carry):
+        for b in range(LOADS):
+            for c in range(0, width, BLOCK):
+                for i, piece in enumerate(split3(panel[b, :, c : c + BLOCK])):
+                    pieces[k * i : k * (i + 1), width * b + c : width * b + c + BLOCK] = piece
+        return carry
+
+    lax.fori_loop(0, jnp.minimum(ii + 1, 1), split_panel, 0)
+    keep = pltpu.make_async_copy(pieces, s_ref, done)
+    keep.start()
     drain(in_1, n_inner - 1, recv.at[1])
     col_2[gi] = pair_sum([in_1[i] for i in range(n_inner)], k)
     share((col_2.at[gi], col_2.at[gi], column + column_mates + sibling, 3))
@@ -205,6 +217,7 @@
     drain(in_2, 2 * n_inner - 1, recv.at[4])
     for c in range(2):
         put(pair_sum([in_2[n_inner * c + i] for i in range(n_inner)], k), quads * c + n_a)
+    keep.wait()
     drain(half, 1, send.at[0])
     drain(in_1, n_inner - 1, send.at[1])
     drain(col_1, depth - 1, send.at[2])
@@ -225,11 +238,18 @@
 
     return pl.pallas_call(
         functools.partial(sum_kernel, n_inner, n_grp),
-        out_shape=jax.ShapeDtypeStruct((rows, 2 * k), F32),
+        out_shape=(
+            jax.ShapeDtypeStruct((rows, 2 * k), F32),
+            jax.ShapeDtypeStruct((3 * k, n), BF16),
+        ),
         in_specs=[pl.BlockSpec(memory_space=pltpu.HBM)],
-        out_specs=pl.BlockSpec(memory_space=pltpu.VMEM),
+        out_specs=(
+            pl.BlockSpec(memory_space=pltpu.VMEM),
+            pl.BlockSpec(memory_space=pltpu.HBM),
+        ),
         scratch_shapes=[
             pltpu.VMEM((LOADS, k, n // LOADS), F32),
+            pltpu.VMEM((3 * k, n), BF16),
             slots(2, quads),
             slots(1, quads),
             slots(n_inner, n_a),
@@ -239,6 +259,7 @@
             pltpu.SemaphoreType.DMA((LOADS,)),
             pltpu.SemaphoreType.DMA((5,)),
             pltpu.SemaphoreType.DMA((5,)),
+            pltpu.SemaphoreType.DMA,
         ],
         compiler_params=pltpu.CompilerParams(collective_id=0, has_side_effects=True),
     )(panel)
@@ -285,7 +306,7 @@
     return jnp.concatenate(rows, axis=0)
 
 
-def first_factor(packed, k, w1_ref, g_ref, unit_ref):
+def first_factor(packed, k):
     r_id = lax.broadcasted_iota(jnp.int32, (k, k), 0)
     c_id = lax.broadcasted_iota(jnp.int32, (k, k), 1)
     eye = r_id == c_id
@@ -299,22 +320,21 @@
 
     col = unit(jnp.sum(diag, axis=1, keepdims=True))
     row = unit(jnp.sum(diag, axis=0, keepdims=True))
-    unit_ref[...] = jnp.broadcast_to(row, unit_ref.shape)
     hi = hi * col * row
     lo = lo * col * row
     top, rest = cut(hi, 4.0, (-7, -15, -23))
     tail, _ = cut(rest + lo, 4.0, (-31, -39, -47))
-    for i, piece in enumerate(top + tail):
-        g_ref[k * i : k * (i + 1), :] = piece
     ident = jnp.where(eye, 1.0, 0.0).astype(F32)
-    w1_ref[...] = eliminate(jnp.concatenate([ident, hi], axis=1), k)[:, :k]
+    w1 = eliminate(jnp.concatenate([ident, hi], axis=1), k)[:, :k]
+    return w1, jnp.concatenate(top + tail, axis=0), row
 
 
 def half_lower(x, r_id, c_id):
     return jnp.where(r_id > c_id, x, jnp.where(r_id == c_id, 0.5 * x, 0.0))
 
 
-def factor(w1, g_stack, row, k, norm, w2_ref, beside):
+def factor(packed, k, norm, w_ref, w2_ref, u_ref, unit_ref):
+    w1, g_stack, row = first_factor(packed, k)
     r_id = lax.broadcasted_iota(jnp.int32, (k, k), 0)
     c_id = lax.broadcasted_iota(jnp.int32, (k, k), 1)
     ident = jnp.where(r_id == c_id, 1.0, 0.0).astype(F32)
@@ -322,7 +342,6 @@
     w_stack = jnp.concatenate(w_pieces, axis=0)
     w1 = w_pieces[0].astype(F32) + w_pieces[1].astype(F32)
     prod = lax.dot_general(g_stack, w_stack, NT, preferred_element_type=F32)
-    beside(0, 3)
     part = [prod[k * i : k * (i + 1), :] for i in range(6)]
     s, e = two_sum(part[0], part[1])
     s, f = two_sum(s, part[2])
@@ -333,7 +352,6 @@
     top, rest = cut(u_hi, u_scale, (-7, -15, -23))
     tail, _ = cut(rest + u_lo, u_scale, (-31, -39))
     part = [lax.dot_general(w_stack, p, NN, preferred_element_type=F32) for p in top + tail]
-    beside(3, 8)
     large = [part[0][:k], part[0][k:], part[1][:k], part[1][k:], part[2][:k]]
     m_lo = part[2][k:] + part[3][:k] + (part[3][k:] + part[4][:k] + part[4][k:])
     m_hi = large[0]
@@ -352,12 +370,14 @@
     def _():
         w2_ref[...] = eliminate(jnp.concatenate([ident, ident + rest], axis=1), k)[:, :k]
 
-    w2 = w2_ref[...]
-    w = lax.dot_general(w2, w1, NN, precision=EXACT, preferred_element_type=F32)
-    tri = lax.dot_general(w2, u_hi, NT, precision=EXACT, preferred_element_type=F32)
-    w = w * (row * norm)
-    tri = jnp.where(c_id >= r_id, tri / (row * norm), 0.0)
-    return w, tri
+    w = lax.dot_general(w2_ref[...], w1, NN, precision=EXACT, preferred_element_type=F32)
+    w0, w1, w2 = split3(w * (row * norm))
+    zero = jnp.zeros_like(w0)
+    w_ref[:k, :] = jnp.concatenate([w0, w0, w0], axis=1)
+    w_ref[k : 2 * k, :] = jnp.concatenate([w1, w1, zero], axis=1)
+    w_ref[2 * k :, :] = jnp.concatenate([w2, zero, zero], axis=1)
+    u_ref[...] = u_hi
+    unit_ref[...] = jnp.broadcast_to(row * norm, unit_ref.shape)
 
 
 def split3(x):
@@ -368,49 +388,39 @@
 
 
 def apply_kernel(
-    norm, p_ref, a_ref, q_ref, t_ref, panel, pieces, out, tri, w1, w2, g_stack, unit, load, store
+    norm, p_ref, s_ref, q_ref, t_ref, pieces, out, tri, w, w2, u, unit, load, store
 ):
-    k, n = a_ref.shape
-    width = n // LOADS
-    loads = []
-    for b in range(LOADS):
-        at = pl.ds(width * b, width)
-        loads.append(pltpu.make_async_copy(a_ref.at[:, at], panel.at[:, at], load.at[b]))
-        loads[-1].start()
+    k, n = q_ref.shape
+    arrival = pltpu.make_async_copy(s_ref, pieces, load)
+    arrival.start()
 
     def one_pass(_, carry):
-        first_factor(p_ref[...], k, w1, g_stack, unit)
+        factor(p_ref[...], k, norm, w, w2, u, unit)
         return carry
 
     lax.fori_loop(0, jnp.minimum(lax.axis_index("inner") + 1, 1), one_pass, 0)
-    for copy in loads:
-        copy.wait()
-
-    def split_blocks(first, last):
-        for b in range(first, last):
-            at = slice(n // 8 * b, n // 8 * (b + 1))
-            for i, piece in enumerate(split3(panel[:, at])):
-                pieces[k * i : k * (i + 1), at] = piece
-
-    w, tri[...] = factor(w1[...], g_stack[...], unit[:1, :], k, norm, w2, split_blocks)
-    stores = [pltpu.make_async_copy(tri, t_ref, store.at[STORES])]
-    stores[0].start()
-    w0, w1, w2 = split3(w)
-    w = jnp.concatenate([w0, w1, w0, w1, w0, w2], axis=1)
+    arrival.wait()
+    stores = []
     width = n // STORES
     for b in range(STORES):
         at = pl.ds(width * b, width)
-        a0, a1, a2 = (pieces[k * i : k * (i + 1), at] for i in range(3))
-        stack = jnp.concatenate([a0, a0, a1, a1, a2, a0], axis=0)
-        out[:, at] = lax.dot_general(w, stack, NN, preferred_element_type=F32)
+        prod = lax.dot_general(w[...], pieces[:, at], NN, preferred_element_type=F32)
+        out[:, at] = prod[:k] + (prod[k : 2 * k] + prod[2 * k :])
         stores.append(pltpu.make_async_copy(out.at[:, at], q_ref.at[:, at], store.at[b]))
         stores[-1].start()
+        if b == 1:
+            r = lax.dot_general(w2[...], u[...], NT, precision=EXACT, preferred_element_type=F32)
+            r_id = lax.broadcasted_iota(jnp.int32, (k, k), 0)
+            c_id = lax.broadcasted_iota(jnp.int32, (k, k), 1)
+            tri[...] = jnp.where(c_id >= r_id, r / unit[:1, :], 0.0)
+            stores.append(pltpu.make_async_copy(tri, t_ref, store.at[STORES]))
+            stores[-1].start()
     for copy in stores:
         copy.wait()
 
 
-def factor_and_apply(g, panel, norm):
-    k, n = panel.shape
+def factor_and_apply(packed, pieces, norm):
+    k, n = pieces.shape[0] // 3, pieces.shape[1]
     whole = pl.BlockSpec(memory_space=pltpu.VMEM)
     stay = pl.BlockSpec(memory_space=pltpu.HBM)
     return pl.pallas_call(
@@ -419,23 +429,23 @@
         in_specs=[whole, stay],
         out_specs=(stay, stay),
         scratch_shapes=[
-            pltpu.VMEM((k, n), F32),
             pltpu.VMEM((3 * k, n), BF16),
             pltpu.VMEM((k, n), F32),
             pltpu.VMEM((k, k), F32),
+            pltpu.VMEM((3 * k, 3 * k), BF16),
             pltpu.VMEM((k, k), F32),
             pltpu.VMEM((k, k), F32),
-            pltpu.VMEM((6 * k, k), BF16),
             pltpu.VMEM((8, k), F32),
-            pltpu.SemaphoreType.DMA((LOADS,)),
+            pltpu.SemaphoreType.DMA,
             pltpu.SemaphoreType.DMA((STORES + 1,)),
         ],
-    )(g, panel)
+    )(packed, pieces)
 
 
 def per_device(panel):
     n_all = panel.shape[1] * lax.axis_size("inner") * lax.axis_size("grp")
-    return factor_and_apply(gram_sum(panel), panel, math.sqrt(n_all))
+    packed, pieces = gram_sum(panel)
+    return factor_and_apply(packed, pieces, math.sqrt(n_all))
 
 
 def solution(mesh):

time: 32 us -> 29.3 us (0.916)
  Pallas kernels: 31.2 us -> 28.5 us
    pallas_call x1, Pallas kernels: 8.6 us -> 5.81 us  [factor_and_apply(): pl.pallas_call(functools.partial(apply_kernel, norm), out_shape=(jax.Shap...]
where the time goes in v6:
time: 29.3 us; the launch traced here: 29.1 us
  Pallas kernels  28.5 us (97%)
  between operations  0.64 us (2%)
    pallas_call x1, Pallas kernels, gram_sum(): pl.pallas_call(functools.partial(sum_kernel, n_inner, n_grp), out_shape=(...  22.7 us
    pallas_call x1, Pallas kernels, factor_and_apply(): pl.pallas_call(functools.partial(apply_kernel, norm), out_shape=(jax.Shap...  5.81 us

profile of v6, /device:TPU:1, one launch (start us, length us, event | category | flops | bytes accessed | tf_op | source)
XLA Modules:
  0.0 29.1 jit_solution(11388533802877062086)
XLA Ops:
  0.6 22.7 %shard_map.30 = (f32[36,128]{1,0:T(8,128)}, bf16[192,8192]{1,0:T(8,128)(2,1)}) custom-call(f32[64,8192]{1,0:T(8,128)} %a_ref.1), custom_call_target="tpu_custom_call" | custom-call | tf_op jit(solution)/shard_map/pallas_call | solution.py:239
  23.3 5.8 %shard_map.31 = (f32[64,8192]{1,0:T(8,128)}, f32[64,64]{1,0:T(8,128)}) custom-call(f32[36,128]{1,0:T(8,128)} %get-tuple-element.4.p_ref, bf16[192,8192]{1,0:T(8,128)(2,1)} %get-tuple-element.5.s_ref), custom_call_target="tpu_custom_call" | custom-call | tf_op jit(solution)/shard_map/pallas_call | solution.py:426

commit v7 on v6

--- a/solution.py
+++ b/solution.py
@@ -363,19 +363,23 @@
     p_16 = p.astype(BF16)
     square = lax.dot_general(p_16, p_16, NN, preferred_element_type=F32)
     gram = lax.dot_general(p_16, p_16, NT, preferred_element_type=F32)
-    w2_ref[...] = ident - p + (square + half_lower(gram, r_id, c_id))
     small = jnp.sum(p * p) < 2.0**-11
+
+    def finish(w2):
+        w2_ref[...] = w2
+        w = lax.dot_general(w2, w1, NN, precision=EXACT, preferred_element_type=F32)
+        pieces = split3(w * (row * norm))
+        zero = jnp.zeros_like(pieces[0])
+        for i in range(3):
+            line = [pieces[i]] * (3 - i) + [zero] * i
+            w_ref[k * i : k * (i + 1), :] = jnp.concatenate(line, axis=1)
+
+    finish(ident - p + (square + half_lower(gram, r_id, c_id)))
 
     @pl.when(jnp.logical_not(small))
     def _():
-        w2_ref[...] = eliminate(jnp.concatenate([ident, ident + rest], axis=1), k)[:, :k]
-
-    w = lax.dot_general(w2_ref[...], w1, NN, precision=EXACT, preferred_element_type=F32)
-    w0, w1, w2 = split3(w * (row * norm))
-    zero = jnp.zeros_like(w0)
-    w_ref[:k, :] = jnp.concatenate([w0, w0, w0], axis=1)
-    w_ref[k : 2 * k, :] = jnp.concatenate([w1, w1, zero], axis=1)
-    w_ref[2 * k :, :] = jnp.concatenate([w2, zero, zero], axis=1)
+        finish(eliminate(jnp.concatenate([ident, ident + rest], axis=1), k)[:, :k])
+
     u_ref[...] = u_hi
     unit_ref[...] = jnp.broadcast_to(row * norm, unit_ref.shape)
 

time: 29.3 us -> 29.3 us (level)
  no operation moved by 1% of the time
where the time goes in v7:
time: 29.3 us; the launch traced here: 29.1 us
  Pallas kernels  28.5 us (97%)
  between operations  0.64 us (2%)
    pallas_call x1, Pallas kernels, gram_sum(): pl.pallas_call(functools.partial(sum_kernel, n_inner, n_grp), out_shape=(...  22.7 us
    pallas_call x1, Pallas kernels, factor_and_apply(): pl.pallas_call(functools.partial(apply_kernel, norm), out_shape=(jax.Shap...  5.8 us

profile of v7, /device:TPU:1, one launch (start us, length us, event | category | flops | bytes accessed | tf_op | source)
XLA Modules:
  0.0 29.1 jit_solution(18188644162327341896)
XLA Ops:
  0.6 22.7 %shard_map.30 = (f32[36,128]{1,0:T(8,128)}, bf16[192,8192]{1,0:T(8,128)(2,1)}) custom-call(f32[64,8192]{1,0:T(8,128)} %a_ref.1), custom_call_target="tpu_custom_call" | custom-call | tf_op jit(solution)/shard_map/pallas_call | solution.py:239
  23.3 5.8 %shard_map.31 = (f32[64,8192]{1,0:T(8,128)}, f32[64,64]{1,0:T(8,128)}) custom-call(f32[36,128]{1,0:T(8,128)} %get-tuple-element.4.p_ref, bf16[192,8192]{1,0:T(8,128)(2,1)} %get-tuple-element.5.s_ref), custom_call_target="tpu_custom_call" | custom-call | tf_op jit(solution)/shard_map/pallas_call | solution.py:430

commit v8 on v7

--- a/solution.py
+++ b/solution.py
@@ -43,7 +43,6 @@
 
 QUAD = 4
 BLOCK = 1024
-LOADS = 2
 STORES = 8
 
 
@@ -115,16 +114,15 @@
     load, send, recv, done
 ):
     k, n = a_ref.shape
-    width = n // LOADS
     ii = lax.axis_index("inner")
     gi = lax.axis_index("grp")
 
-    def arrival(b):
-        at = pl.ds(width * b, width)
-        return pltpu.make_async_copy(a_ref.at[:, at], panel.at[b], load.at[b])
-
-    for b in range(LOADS):
-        arrival(b).start()
+    edges = (0, (n // BLOCK * 3 // 8) * BLOCK, n)
+    loads = []
+    for b in range(2):
+        at = pl.ds(edges[b], edges[b + 1] - edges[b])
+        loads.append(pltpu.make_async_copy(a_ref.at[:, at], panel.at[:, at], load.at[b]))
+        loads[-1].start()
 
     side, depth = math.isqrt(n_inner), n_grp // 2
     y, x = lax.div(ii, side), lax.rem(ii, side)
@@ -149,14 +147,20 @@
     for _, to in sorted(everyone, key=lambda p: -p[0]):
         pl.semaphore_signal(barrier, inc=1, device_id=to, device_id_type=mesh_id)
 
-    def add_copy(b, sums):
-        arrival(b).wait()
-        for c in range(width // BLOCK):
-            sums = add_products(panel[b, :, BLOCK * c : BLOCK * (c + 1)], sums, k)
-        return sums
-
+    def add_copy(b):
+        def add(_, sums):
+            loads[b].wait()
+            for c in range(edges[b], edges[b + 1], BLOCK):
+                sums = add_products(panel[:, c : c + BLOCK], sums, k)
+            return sums
+
+        return add
+
+    one = jnp.minimum(ii + 1, 1)
     zeros = jnp.zeros((k, 2 * k), F32)
-    sums = lax.fori_loop(0, LOADS, add_copy, (zeros,) * 5 + (zeros[:, :k],))
+    sums = (zeros,) * 5 + (zeros[:, :k],)
+    for b in range(2):
+        sums = lax.fori_loop(0, one, add_copy(b), sums)
     body, diag = fold(join_products(sums, k), k)
     quads = halves.shape[1]
     n_a, n_b = in_1.shape[1], col_1.shape[1]
@@ -189,13 +193,12 @@
     share((in_1.at[ii], in_1.at[ii], plane, 1), (col_1.at[level], col_1.at[level], column, 2))
 
     def split_panel(_, carry):
-        for b in range(LOADS):
-            for c in range(0, width, BLOCK):
-                for i, piece in enumerate(split3(panel[b, :, c : c + BLOCK])):
-                    pieces[k * i : k * (i + 1), width * b + c : width * b + c + BLOCK] = piece
+        for c in range(0, n, BLOCK):
+            for i, piece in enumerate(split3(panel[:, c : c + BLOCK])):
+                pieces[k * i : k * (i + 1), c : c + BLOCK] = piece
         return carry
 
-    lax.fori_loop(0, jnp.minimum(ii + 1, 1), split_panel, 0)
+    lax.fori_loop(0, one, split_panel, 0)
     keep = pltpu.make_async_copy(pieces, s_ref, done)
     keep.start()
     drain(in_1, n_inner - 1, recv.at[1])
@@ -248,7 +251,7 @@
             pl.BlockSpec(memory_space=pltpu.HBM),
         ),
         scratch_shapes=[
-            pltpu.VMEM((LOADS, k, n // LOADS), F32),
+            pltpu.VMEM((k, n), F32),
             pltpu.VMEM((3 * k, n), BF16),
             slots(2, quads),
             slots(1, quads),
@@ -256,7 +259,7 @@
             slots(n_grp // 2, n_b),
             slots(n_grp, n_a),
             slots(2 * n_inner, n_b),
-            pltpu.SemaphoreType.DMA((LOADS,)),
+            pltpu.SemaphoreType.DMA((2,)),
             pltpu.SemaphoreType.DMA((5,)),
             pltpu.SemaphoreType.DMA((5,)),
             pltpu.SemaphoreType.DMA,

time: 29.3 us -> 29.3 us (level)
  no operation moved by 1% of the time
where the time goes in v8:
time: 29.3 us; the launch traced here: 29.1 us
  Pallas kernels  28.5 us (97%)
  between operations  0.64 us (2%)
    pallas_call x1, Pallas kernels, gram_sum(): pl.pallas_call(functools.partial(sum_kernel, n_inner, n_grp), out_shape=(...  22.7 us
    pallas_call x1, Pallas kernels, factor_and_apply(): pl.pallas_call(functools.partial(apply_kernel, norm), out_shape=(jax.Shap...  5.8 us

profile of v8, /device:TPU:1, one launch (start us, length us, event | category | flops | bytes accessed | tf_op | source)
XLA Modules:
  0.0 29.1 jit_solution(7540769492314602330)
XLA Ops:
  0.6 22.7 %shard_map.30 = (f32[36,128]{1,0:T(8,128)}, bf16[192,8192]{1,0:T(8,128)(2,1)}) custom-call(f32[64,8192]{1,0:T(8,128)} %a_ref.1), custom_call_target="tpu_custom_call" | custom-call | tf_op jit(solution)/shard_map/pallas_call | solution.py:242
  23.3 5.8 %shard_map.31 = (f32[64,8192]{1,0:T(8,128)}, f32[64,64]{1,0:T(8,128)}) custom-call(f32[36,128]{1,0:T(8,128)} %get-tuple-element.4.p_ref, bf16[192,8192]{1,0:T(8,128)(2,1)} %get-tuple-element.5.s_ref), custom_call_target="tpu_custom_call" | custom-call | tf_op jit(solution)/shard_map/pallas_call | solution.py:433
